TPU v7x, 128 devices: a whole 4x4x4 slice. The times are simulated.
128 devices in a mesh: gx: 8 (over y_hi, x), gy: 16 (over z, y_lo, core).
Axes of the slice: x: 4, y: 4 (y_hi: 2, y_lo: 2; y = y_hi * 2 + y_lo), z: 4, core: 2. Of those that a mesh axis runs over, the one named last changes fastest.
Arguments:
- resid: bfloat16 [1024, 16384], P('gx', 'gy'), may hold values from -6 to 6
- queries: bfloat16 [1024, 16384], P('gy', 'gx'), may hold values from -480 to 480
- tree_kv: bfloat16 [1024, 2048], P('gy', 'gx'), may hold values from -6 to 6
- cache: bfloat16 [8, 128, 128, 256], P('gx', 'gy'), may hold values from -6 to 6
- page_table: int32 [16, 8], P('gy'), may hold values from 0 to 7, as said below
- cache_len: int32 [16], P('gy'), may hold values from 128 to 1024
- tree_size: int32 [16], P('gy'), may hold values from 16 to 64
- parents: int32 [16, 64], P('gy'), may hold values from -1 to 62, as said below
- w_out: bfloat16 [16384, 16384], P('gx', 'gy'), may hold values from -0.046875 to 0.046875
- gain: bfloat16 [16384], P('gy'), may hold values from 0.099609375 to 1.8984375
- w_gate: bfloat16 [16384, 26624], P('gy', 'gx'), may hold values from -0.046875 to 0.046875
- w_up: bfloat16 [16384, 26624], P('gy', 'gx'), may hold values from -0.046875 to 0.046875
- w_down: bfloat16 [26624, 16384], P('gx', 'gy'), may hold values from -0.0390625 to 0.0390625
Outputs:
- layer_out: bfloat16 [1024, 16384], P('gx', 'gy')
Inputs may be any that keep to these rules, and one draw needn't show every extreme that they name: `page_table`: the one request r held at an index of gy names each of the 8 pages of that index exactly once. parents[r, 0] is -1 and parents[r, n] lies in 0 to n - 1 for n >= 1.
All inputs are finite; a program needn't handle non-finite values.
Results may differ from a plain program's by a relative error of at most 0.025.
Values may be sent and summed in bfloat16 or wider, within the bound.
A program may use at most 192 MiB of HBM per device.

v0:
```python
import jax
import jax.numpy as jnp
from jax import lax
from jax.sharding import PartitionSpec as P

D = 16384
HQ = 128
KVH = 8
HD = 128
MAXTREE = 64
PAGE = 128
MAXPAGES = 8


EPSILON = 1e-05


def ancestry(parent_row, tree_len):
    nodes = jnp.arange(MAXTREE, dtype=jnp.int32)
    linked = (parent_row[:, None] == nodes[None, :]).astype(jnp.float32)
    reach = jnp.eye(MAXTREE, dtype=jnp.float32) + linked
    for sweep in range(max(1, (MAXTREE - 1).bit_length())):
        reach = jnp.minimum(jnp.dot(reach, reach, precision=lax.Precision.HIGHEST), 1.0)
    return (reach > 0.5) & (nodes[None, :] < tree_len)


def attend(query_rows, tree_rows, context, ctx_len, tree_len, parent_row):
    groups = HQ // KVH
    scale = HD ** (-0.5)
    allowed_tree = ancestry(parent_row, tree_len)[:, None, :]
    positions = jnp.arange(context.shape[1], dtype=jnp.int32)
    allowed_ctx = (positions < ctx_len)[None, None, :]
    live = (jnp.arange(MAXTREE, dtype=jnp.int32) < tree_len)[:, None, None]
    q_block = query_rows.reshape(MAXTREE, groups, HD)
    tree_keys = tree_rows[:, 0:HD]
    tree_vals = tree_rows[:, HD : 2 * HD]
    ctx_keys = context[0, :, :HD]
    ctx_vals = context[0, :, HD:]
    ctx_scores = (
        jnp.einsum("ngd,td->ngt", q_block, ctx_keys, preferred_element_type=jnp.float32) * scale
    )
    tree_scores = (
        jnp.einsum("ngd,md->ngm", q_block, tree_keys, preferred_element_type=jnp.float32) * scale
    )
    ctx_scores = jnp.where(allowed_ctx, ctx_scores, -1e30)
    tree_scores = jnp.where(allowed_tree, tree_scores, -1e30)
    row_max = jnp.maximum(
        jnp.max(ctx_scores, axis=-1, keepdims=True), jnp.max(tree_scores, axis=-1, keepdims=True)
    )
    ctx_exp = jnp.exp(ctx_scores - row_max)
    tree_exp = jnp.exp(tree_scores - row_max)
    total = jnp.sum(ctx_exp, axis=-1, keepdims=True) + jnp.sum(tree_exp, axis=-1, keepdims=True)
    ctx_probs = (ctx_exp / total).astype(jnp.bfloat16)
    tree_probs = (tree_exp / total).astype(jnp.bfloat16)
    mixed = jnp.einsum("ngt,td->ngd", ctx_probs, ctx_vals, preferred_element_type=jnp.float32)
    mixed = mixed + jnp.einsum(
        "ngm,md->ngd", tree_probs, tree_vals, preferred_element_type=jnp.float32
    )
    mixed = jnp.where(live, mixed, 0.0)
    outputs = mixed.astype(jnp.bfloat16).reshape(MAXTREE, groups * HD)
    return outputs


def body(
    resid,
    queries,
    tree_kv,
    cache,
    page_table,
    cache_len,
    tree_size,
    parents,
    w_out,
    gain,
    w_gate,
    w_up,
    w_down,
):
    local_heads = cache.shape[0]
    context = jnp.take(cache, page_table[0], axis=1).reshape(local_heads, MAXPAGES * PAGE, 2 * HD)
    attn_parts = attend(queries, tree_kv, context, cache_len[0], tree_size[0], parents[0])
    all_attn = lax.all_gather(attn_parts, "gy", axis=0, tiled=True)
    rows = all_attn
    projected = lax.psum_scatter(
        jnp.dot(rows, w_out, preferred_element_type=jnp.float32).astype(jnp.bfloat16),
        "gx",
        scatter_dimension=0,
        tiled=True,
    ).astype(jnp.float32)
    hid = (resid.astype(jnp.float32) + projected).astype(jnp.bfloat16)
    hid_wide = hid.astype(jnp.float32)
    square_total = lax.psum(jnp.sum(hid_wide * hid_wide, axis=1), "gy")
    mean_sq = (square_total / D)[:, None]
    normed = (hid_wide * lax.rsqrt(mean_sq + EPSILON) * gain.astype(jnp.float32)[None, :]).astype(
        jnp.bfloat16
    )
    local_units = w_gate.shape[1]
    shard_rows = lax.all_gather(normed, "gx", axis=0, tiled=True)
    gate_part = jnp.dot(shard_rows, w_gate, preferred_element_type=jnp.float32)
    up_part = jnp.dot(shard_rows, w_up, preferred_element_type=jnp.float32)
    partial_units = jnp.concatenate([gate_part, up_part], axis=1)
    unit_share = lax.psum_scatter(
        partial_units.astype(jnp.bfloat16), "gy", scatter_dimension=0, tiled=True
    ).astype(jnp.float32)
    hidden_share = (jax.nn.silu(unit_share[:, :local_units]) * unit_share[:, local_units:]).astype(
        jnp.bfloat16
    )
    all_hidden = lax.all_gather(hidden_share, "gy", axis=0, tiled=True)
    rows = all_hidden
    down = lax.psum_scatter(
        jnp.dot(rows, w_down, preferred_element_type=jnp.float32).astype(jnp.bfloat16),
        "gx",
        scatter_dimension=0,
        tiled=True,
    ).astype(jnp.float32)
    return (hid_wide + down).astype(jnp.bfloat16)


def solution(mesh):
    in_specs = (
        P("gx", "gy"),
        P("gy", "gx"),
        P("gy", "gx"),
        P("gx", "gy", None, None),
        P("gy", None),
        P("gy"),
        P("gy"),
        P("gy", None),
        P("gx", "gy"),
        P("gy"),
        P("gy", "gx"),
        P("gy", "gx"),
        P("gx", "gy"),
    )
    out_specs = P("gx", "gy")
    return jax.shard_map(body, mesh=mesh, in_specs=in_specs, out_specs=out_specs, check_vma=False)
```

profile of v0, /device:TPU:0, one launch (start us, length us, event | category | flops | bytes accessed | tf_op | source)
XLA Modules:
  0.0 556.6 jit_solution(4600812987481769741)
XLA Ops:
  6.5 0.7 fusion.27
  7.3 0.7 compare_and_fusion
  9.3 1.0 convolution_minimum_fusion.5
  11.0 1.0 copy.39
  12.2 1.1 fusion.30
  13.3 0.6 gather_fusion
  13.9 0.2 bitcast_select_fusion
  14.1 2.7 bitcast_reduce_fusion
  16.9 3.2 fusion.1
  20.1 0.4 fusion.14
  20.5 3.3 fusion.2
  23.9 0.3 divide_convert_fusion.2
  24.3 0.2 fusion.6
  24.5 0.8 copy.49
  25.4 40.0 %all-gather.4.cloned.1.call-done = bf16[1024,2048]{1,0:T(8,128)(2,1)} async-done(((bf16[64,2048]{1,0:T(8,128)(2,1)}), bf16[1024,2048]{1,0:T(8,128)(2,1)}) %all-gather.4.cloned.1.call-update) | async-done | bytes 4194320 | tf_op jit(solution)/shard_map/all_gather | solution.py:82
  65.4 9.3 %convolution_convert_fusion.3 = bf16[1024,1024]{1,0:T(8,128)(2,1)} fusion(bf16[1024,2048]{1,0:T(8,128)(2,1)} %all-gather.4.cloned.1.call-done, bf16[2048,1024]{1,0:T(8,128)(2,1)} %param.21), kind=kOutput, calls=%fused_computation.12 | convolution fusion | flops 4296015872 | bytes 10485760 | tf_op jit(solution)/shard_map/dot_general | solution.py:85
  74.7 75.4 %reduce-scatter.4.cloned.1.call-done = bf16[128,1024]{1,0:T(8,128)(2,1)} async-done(((bf16[1024,1024]{1,0:T(8,128)(2,1)}), bf16[128,1024]{1,0:T(8,128)(2,1)}) %reduce-scatter.4.cloned.1.call-update) | async-done | bytes 262160 | tf_op jit(solution)/shard_map/reduce_scatter | solution.py:84
  150.1 1.1 fusion.10
  151.2 28.0 %psum.7 = f32[128]{0:T(128)S(1)} all-reduce(f32[128]{0:T(128)S(1)} %fusion.10), channel_id=1, replica_groups=mesh['gx'=8,'gy'=16] {'gy'}, use_global_device_ids=true, to_apply=%region_6.7 | all-reduce | flops 128 | bytes 1024 | tf_op jit(solution)/shard_map/psum | solution.py:92
  179.2 1.8 fusion.12
  181.0 0.2 reduce-scatter.6.cloned.1.call-start
  181.3 51.6 %all-gather.6.cloned.1.call-done = bf16[1024,1024]{1,0:T(8,128)(2,1)} async-done(((bf16[128,1024]{1,0:T(8,128)(2,1)}), bf16[1024,1024]{1,0:T(8,128)(2,1)}) %all-gather.6.cloned.1.call-update) | async-done | bytes 2097168 | tf_op jit(solution)/shard_map/all_gather | solution.py:98
  232.9 10.8 %convolution_convert_fusion = bf16[1024,3328]{1,0:T(8,128)(2,1)S(1)} fusion(bf16[1024,1024]{1,0:T(8,128)(2,1)} %all-gather.6.cloned.1.call-done, bf16[1024,3328]{1,0:T(8,128)(2,1)} %param.24), kind=kOutput, calls=%fused_computation.2 | convolution fusion | flops 6982729728 | bytes 15728640 | tf_op jit(solution)/shard_map/dot_general | solution.py:100
  243.7 10.6 %convolution_convert_fusion.1 = bf16[1024,3328]{1,0:T(8,128)(2,1)S(1)} fusion(bf16[1024,1024]{1,0:T(8,128)(2,1)S(1)} %copy-done.7, bf16[1024,3328]{1,0:T(8,128)(2,1)} %param.23), kind=kOutput, calls=%fused_computation.3 | convolution fusion | flops 6982729728 | bytes 15728640 | tf_op jit(solution)/shard_map/dot_general | solution.py:99
  254.4 9.0 %pad_maximum_fusion = bf16[1024,6656]{1,0:T(8,128)(2,1)} fusion(bf16[1024,3328]{1,0:T(8,128)(2,1)S(1)} %convolution_convert_fusion, bf16[1024,3328]{1,0:T(8,128)(2,1)S(1)} %convolution_convert_fusion.1), kind=kLoop, calls=%fused_computation.1 | loop fusion | flops 27262976 | bytes 27262976 | tf_op jit(solution)/shard_map/concatenate | solution.py:101
  263.4 149.8 %reduce-scatter.6.cloned.1.call-done = bf16[64,6656]{1,0:T(8,128)(2,1)} async-done(((bf16[1024,6656]{1,0:T(8,128)(2,1)}), bf16[64,6656]{1,0:T(8,128)(2,1)}) %reduce-scatter.6.cloned.1.call-update) | async-done | bytes 851984 | tf_op jit(solution)/shard_map/reduce_scatter | solution.py:102
  413.2 1.3 convert_element_type.64
  414.5 1.0 fusion.9
  415.6 43.4 %all-gather.8.cloned.1.call-done = bf16[1024,3328]{1,0:T(8,128)(2,1)} async-done(((bf16[64,3328]{1,0:T(8,128)(2,1)}), bf16[1024,3328]{1,0:T(8,128)(2,1)}) %all-gather.8.cloned.1.call-update) | async-done | bytes 6815760 | tf_op jit(solution)/shard_map/all_gather | solution.py:108
  459.0 12.5 %convolution_convert_fusion.2 = bf16[1024,1024]{1,0:T(8,128)(2,1)} fusion(bf16[1024,3328]{1,0:T(8,128)(2,1)} %all-gather.8.cloned.1.call-done, bf16[3328,1024]{1,0:T(8,128)(2,1)} %param.25), kind=kOutput, calls=%fused_computation.11 | convolution fusion | flops 6980370432 | bytes 15728640 | tf_op jit(solution)/shard_map/dot_general | solution.py:111
  471.5 76.5 %reduce-scatter.8.cloned.1.call-done = bf16[128,1024]{1,0:T(8,128)(2,1)} async-done(((bf16[1024,1024]{1,0:T(8,128)(2,1)}), bf16[128,1024]{1,0:T(8,128)(2,1)}) %reduce-scatter.8.cloned.1.call-update) | async-done | bytes 262160 | tf_op jit(solution)/shard_map/reduce_scatter | solution.py:110
  548.0 1.8 fusion.13
  (44 shorter events, 1.5 us)
Async XLA Ops:
  6.5 6.8 %copy-start = (bf16[1,8,128,256]{3,2,1,0:T(8,128)(2,1)S(1)}, bf16[1,8,128,256]{3,2,1,0:T(8,128)(2,1)}, u32[]{:S(2)}) copy-start(bf16[1,8,128,256]{3,2,1,0:T(8,128)(2,1)} %param.16) | copy-start | bytes 1572868
  6.5 7.6 %copy-start.4 = (bf16[64,2048]{1,0:T(8,128)(2,1)S(1)}, bf16[64,2048]{1,0:T(8,128)(2,1)}, u32[]{:S(2)}) copy-start(bf16[64,2048]{1,0:T(8,128)(2,1)} %param.14) | copy-start | bytes 786436
  6.5 58.8 %all-gather.4.cloned.1.call-start = ((), (), s32[]{:S(2)}) async-start(), calls=%async_computation.3 | async-start | bytes 4456448 | tf_op jit(solution)/shard_map/all_gather | solution.py:82
  20.5 3.8 copy-start.5
  25.3 49.4 %copy-start.6 = (bf16[1024]{0:T(1024)(128)(2,1)S(1)}, bf16[1024]{0:T(1024)(128)(2,1)}, u32[]{:S(2)}) copy-start(bf16[1024]{0:T(1024)(128)(2,1)} %param.22) | copy-start | bytes 6148
  25.3 124.8 %copy-start.2 = (bf16[128,1024]{1,0:T(8,128)(2,1)S(1)}, bf16[128,1024]{1,0:T(8,128)(2,1)}, u32[]{:S(2)}) copy-start(bf16[128,1024]{1,0:T(8,128)(2,1)} %param.13) | copy-start | bytes 786436
  25.3 124.8 %reduce-scatter.4.cloned.1.call-start = ((), (), s32[]{:S(2)}) async-start(), calls=%async_computation.4 | async-start | bytes 2359296 | tf_op jit(solution)/shard_map/reduce_scatter | solution.py:84
  74.7 158.2 %all-gather.6.cloned.1.call-start = ((), (), s32[]{:S(2)}) async-start(), calls=%async_computation.5 | async-start | bytes 2359296 | tf_op jit(solution)/shard_map/all_gather | solution.py:98
  181.0 232.2 %reduce-scatter.6.cloned.1.call-start = ((), (), s32[]{:S(2)}) async-start(), calls=%async_computation.6 | async-start | bytes 14483456 | tf_op jit(solution)/shard_map/reduce_scatter | solution.py:102
  232.9 10.8 %copy-start.7 = (bf16[1024,1024]{1,0:T(8,128)(2,1)S(1)}, bf16[1024,1024]{1,0:T(8,128)(2,1)}, u32[]{:S(2)}) copy-start(bf16[1024,1024]{1,0:T(8,128)(2,1)} %all-gather.6.cloned.1.call-done) | copy-start | bytes 6291460
  263.3 195.7 %all-gather.8.cloned.1.call-start = ((), (), s32[]{:S(2)}) async-start(), calls=%async_computation.7 | async-start | bytes 7241728 | tf_op jit(solution)/shard_map/all_gather | solution.py:108
  415.5 132.5 %copy-start.3 = (bf16[128,1024]{1,0:T(8,128)(2,1)S(1)}, bf16[128,1024]{1,0:T(8,128)(2,1)}, u32[]{:S(2)}) copy-start(bf16[128,1024]{1,0:T(8,128)(2,1)} %reduce-scatter.4.cloned.1.call-done) | copy-start | bytes 786436
  415.5 132.5 %reduce-scatter.8.cloned.1.call-start = ((), (), s32[]{:S(2)}) async-start(), calls=%async_computation.8 | async-start | bytes 2359296 | tf_op jit(solution)/shard_map/reduce_scatter | solution.py:110
  459.0 90.8 %copy-start.1 = (bf16[1,8,128,256]{3,2,1,0:T(8,128)(2,1)S(1)}, bf16[1,8,128,256]{3,2,1,0:T(8,128)(2,1)}, u32[]{:S(2)}) copy-start(bf16[1,8,128,256]{3,2,1,0:T(8,128)(2,1)} %param.16) | copy-start | bytes 1572868
Sparse Core Ops, SparseCore 0:
  25.4 39.8 all-gather.3
  74.8 75.2 reduce-scatter.3
  181.1 51.6 all-gather.5
  263.5 149.6 reduce-scatter.5
  415.6 43.3 all-gather.7
  471.6 76.3 reduce-scatter.7
where the time goes:
time: 557 us
  waiting for transfers between devices  437 us (78%)
  matrix products  52.3 us (9%)
  blocking collectives  28 us (5%)
  other arithmetic  21.4 us (4%)
  between operations  15 us (3%)
    reduce_scatter x1, waiting for transfers between devices, body(): lax.psum_scatter(partial_units.astype(jnp.bfloat16), 'gy', scatter_dimens...  150 us
    reduce_scatter x1, waiting for transfers between devices, body(): lax.psum_scatter(jnp.dot(rows, w_down, preferred_element_type=jnp.float32...  76.5 us
    reduce_scatter x1, waiting for transfers between devices, body(): lax.psum_scatter(jnp.dot(rows, w_out, preferred_element_type=jnp.float32)...  75.4 us
    all_gather x1, waiting for transfers between devices, body(): shard_rows = lax.all_gather(normed, 'gx', axis=0, tiled=True)  51.6 us
    all_gather x1, waiting for transfers between devices, body(): all_hidden = lax.all_gather(hidden_share, 'gy', axis=0, tiled=True)  43.4 us
    all_gather x1, waiting for transfers between devices, body(): all_attn = lax.all_gather(attn_parts, 'gy', axis=0, tiled=True)  40 us
    psum x1, blocking collectives, body(): square_total = lax.psum(jnp.sum(hid_wide * hid_wide, axis=1), 'gy')  28 us
    dot_general x1, matrix products, body(): jnp.dot(rows, w_down, preferred_element_type=jnp.float32)  12.5 us
  transfers between devices with their start and end apart: 6, of which 6 were waited for; matrix products, arithmetic and copies ran while one was open for 0% of the time, Pallas kernels for 0%

commit v1 on v0

v1 whole, which is shorter than its diff:
```python
import jax
import jax.numpy as jnp
from jax import lax
from jax.experimental import pallas as pl
from jax.experimental.pallas import tpu as pltpu
from jax.sharding import PartitionSpec as P

D = 16384
HD = 128
MAXTREE = 64
PAGE = 128
MAXPAGES = 8
EPSILON = 1e-05

MESH = pl.DeviceIdType.MESH
BF = jnp.bfloat16
F32 = jnp.float32

CHUNKS = 4
NODES = MAXTREE // CHUNKS
BLOCK = 2 * NODES
ROWS = 8 * BLOCK
LANES = 128
TILE = 256


def visible_nodes(parents, tree_len):
    shape = (MAXTREE, MAXTREE)
    column, row = lax.broadcasted_iota(jnp.int32, shape, 1), lax.broadcasted_iota(jnp.int32, shape, 0)
    eye = jnp.where(row == column, 1.0, 0.0)
    reach = eye + jnp.where(parents == row, 1.0, 0.0)
    for sweep in range((MAXTREE - 1).bit_length()):
        held = reach.astype(BF)
        reach = jnp.minimum(jnp.dot(held, held, preferred_element_type=F32), 1.0)
    turned = lax.dot_general(
        reach.astype(BF), eye.astype(BF), (((0,), (0,)), ((), ())), preferred_element_type=F32
    )
    return jnp.where(column < tree_len, turned, 0.0)


def attend(query, visible, live, cached, tree_kv, cache, page_table):
    heads = query.shape[1] // HD
    keys = jnp.concatenate([query[:, h * HD : (h + 1) * HD] for h in range(heads)], axis=0)
    contract = (((1,), (1,)), ((), ()))
    context = cache[0].reshape(MAXPAGES * PAGE, 2 * HD)
    scale = HD ** (-0.5)
    ctx_scores = lax.dot_general(keys, context[:, 0:HD], contract, preferred_element_type=F32) * scale
    tree_scores = lax.dot_general(keys, tree_kv[:, 0:HD], contract, preferred_element_type=F32) * scale
    offset = lax.broadcasted_iota(jnp.int32, (1, PAGE), 1)
    bounds = []
    for page in range(MAXPAGES):
        place = jnp.int32(0)
        for p in range(1, MAXPAGES):
            place = jnp.where(page_table[0, p] == page, p, place)
        bounds.append(offset < cached - place * PAGE)
    allowed = jnp.concatenate([jnp.where(bound, 1.0, 0.0) for bound in bounds], axis=1)
    ctx_scores = jnp.where(allowed > 0.5, ctx_scores, -1e30)
    seen = jnp.concatenate([visible] * heads, axis=0)
    tree_scores = jnp.where(seen > 0.5, tree_scores, -1e30)
    row_max = jnp.maximum(
        jnp.max(ctx_scores, axis=-1, keepdims=True), jnp.max(tree_scores, axis=-1, keepdims=True)
    )
    ctx_exp = jnp.exp(ctx_scores - row_max)
    tree_exp = jnp.exp(tree_scores - row_max)
    total = jnp.sum(ctx_exp, axis=-1, keepdims=True) + jnp.sum(tree_exp, axis=-1, keepdims=True)
    share = 1.0 / total
    mixed = jnp.dot((ctx_exp * share).astype(BF), context[:, HD:], preferred_element_type=F32)
    mixed += jnp.dot((tree_exp * share).astype(BF), tree_kv[:, HD:], preferred_element_type=F32)
    count = query.shape[0]
    parts = [jnp.where(live, mixed[h * count : (h + 1) * count, :], 0.0).astype(BF) for h in range(heads)]
    return jnp.concatenate(parts, axis=1)


def remote(src, dst, send_sem, recv_sem, device):
    return pltpu.make_async_remote_copy(
        src_ref=src,
        dst_ref=dst,
        send_sem=send_sem,
        recv_sem=recv_sem,
        device_id=device,
        device_id_type=MESH,
    )


class Place:
    def __init__(self, r, p, prev, follow, pair, sib, core, index):
        self.r, self.p = r, p
        self.prev, self.follow, self.pair, self.sib = prev, follow, pair, sib
        self.core = core
        self.index = index

    def block(self, p, shift):
        return self.index(p, lax.rem(self.r + (4 + shift), 4))


class Scatter:
    def __init__(self, place, part, far, near, last, send, recv):
        self.at = place
        self.part, self.far, self.near, self.last = part, far, near, last
        self.send, self.recv = send, recv
        self.open = {}

    def push(self, k, src, dst, sem, device):
        copy = remote(src, dst, self.send.at[k, sem], self.recv.at[k, sem], device)
        copy.start()
        self.open.setdefault(k, []).append(copy)

    def arrived(self, k, ref, sem):
        remote(ref, ref, self.send.at[k, sem], self.recv.at[k, sem], self.at.pair).wait_recv()

    def step1(self, k):
        at, part = self.at, self.part(k)
        self.push(k, part.at[at.block(0, 2)], self.far.at[k, 0], 0, at.follow)
        self.push(k, part.at[at.block(1, 2)], self.far.at[k, 1], 1, at.prev)
        self.push(k, part.at[at.block(1, 1)], self.near.at[k, 0, 1], 3, at.follow)
        self.push(k, part.at[at.block(0, -1)], self.near.at[k, 1, 0], 4, at.prev)

    def step2(self, k):
        at, part = self.at, self.part(k)
        for way, (p, shift, device, sem) in enumerate(((0, 1, at.follow, 2), (1, -1, at.prev, 5))):
            self.arrived(k, self.far.at[k, way], way)
            mine = at.block(p, shift)
            part[mine] = (part[mine].astype(F32) + self.far[k, way].astype(F32)).astype(BF)
            self.push(k, part.at[mine], self.near.at[k, way, p], sem, device)

    def ring_sum(self, k, p):
        part = self.part(k)
        for way in (0, 1):
            self.arrived(k, self.near.at[k, way, p], 2 + 2 * way + p)
        return (
            part[self.at.block(p, 0)].astype(F32)
            + self.near[k, 0, p].astype(F32)
            + self.near[k, 1, p].astype(F32)
        )

    def step3(self, k):
        at, part = self.at, self.part(k)
        other = 1 - at.p
        theirs = at.block(other, 0)
        part[theirs] = self.ring_sum(k, other).astype(BF)
        self.push(k, part.at[theirs], self.last.at[k], 6, at.pair)

    def step4(self, k):
        total = self.ring_sum(k, self.at.p)
        self.arrived(k, self.last.at[k], 6)
        return total + self.last[k].astype(F32)

    def close(self, k):
        for copy in self.open.pop(k, []):
            copy.wait_send()


class Gather:
    def __init__(self, place, ref, send, recv):
        self.at, self.ref = place, ref
        self.send, self.recv = send, recv
        self.open = {}

    def push(self, k, block, sem, device):
        ref = self.ref(k, self.at.core, block)
        copy = remote(ref, ref, self.send.at[k, sem], self.recv.at[k, sem], device)
        copy.start()
        self.open.setdefault(k, []).append(copy)

    def arrived(self, k, block, sem, core):
        ref = self.ref(k, core, block)
        remote(ref, ref, self.send.at[k, sem], self.recv.at[k, sem], self.at.pair).wait_recv()

    def share(self, k, block):
        self.push(k, block, 7 + block, self.at.sib)

    def step1(self, k):
        at = self.at
        mine = at.block(at.p, 0)
        self.push(k, mine, 0, at.pair)
        self.push(k, mine, 1 + at.p, at.follow)
        self.push(k, mine, 3 + at.p, at.prev)
        self.share(k, mine)

    def step2(self, k):
        at = self.at
        other = 1 - at.p
        block = at.block(other, 0)
        self.arrived(k, block, 0, at.core)
        self.push(k, block, 1 + other, at.follow)
        self.push(k, block, 3 + other, at.prev)
        self.share(k, block)

    def step3(self, k):
        at = self.at
        left, right = at.block(0, -1), at.block(1, 1)
        self.arrived(k, left, 1, at.core)
        self.push(k, left, 5, at.follow)
        self.share(k, left)
        self.arrived(k, right, 4, at.core)
        self.push(k, right, 6, at.prev)
        self.share(k, right)
        left, right = at.block(1, -1), at.block(0, 1)
        self.arrived(k, left, 2, at.core)
        self.share(k, left)
        self.arrived(k, right, 3, at.core)
        self.share(k, right)

    def step4(self, k):
        at = self.at
        left, right = at.block(0, -2), at.block(1, 2)
        self.arrived(k, left, 5, at.core)
        self.share(k, left)
        self.arrived(k, right, 6, at.core)
        self.share(k, right)

    def step5(self, k):
        for block in range(8):
            self.arrived(k, block, 7 + block, 1 - self.at.core)

    def close(self, k):
        for copy in self.open.pop(k, []):
            copy.wait_send()


def layer_kernel(
    page_table,
    cache_len,
    tree_size,
    parents,
    queries,
    tree_kv,
    cache,
    resid,
    gain,
    w_out,
    w_gate,
    w_up,
    w_down,
    out,
    wo,
    wgu,
    wd,
    attn_all,
    proj,
    hid,
    normed_all,
    sums,
    hidden_all,
    visible,
    far_a,
    near_a,
    last_a,
    far_b,
    near_b,
    last_b,
    far_c,
    near_c,
    last_c,
    load_sem,
    swap_send,
    swap_recv,
    ga_send,
    ga_recv,
    gb_send,
    gb_recv,
    gc_send,
    gc_recv,
    sa_send,
    sa_recv,
    sb_send,
    sb_recv,
    sc_send,
    sc_recv,
):
    gx, gy = lax.axis_index("gx"), lax.axis_index("gy")
    yh, x = lax.div(gx, 4), lax.rem(gx, 4)
    z, yl, core = lax.div(gy, 4), lax.rem(lax.div(gy, 2), 2), lax.rem(gy, 2)
    width = wo.shape[1]
    half = wgu.shape[1] // 2
    depth = w_gate.shape[0]

    sib = (gx, z * 4 + yl * 2 + (1 - core))
    along_x = Place(
        x,
        yh,
        (yh * 4 + lax.rem(x + 3, 4), gy),
        (yh * 4 + lax.rem(x + 1, 4), gy),
        ((1 - yh) * 4 + x, gy),
        sib,
        core,
        lambda p, r: p * 4 + r,
    )
    along_z = Place(
        z,
        yl,
        (gx, lax.rem(z + 3, 4) * 4 + yl * 2 + core),
        (gx, lax.rem(z + 1, 4) * 4 + yl * 2 + core),
        (gx, z * 4 + (1 - yl) * 2 + core),
        sib,
        core,
        lambda p, r: r * 2 + p,
    )

    loads = []

    def load(src, dst):
        copy = pltpu.make_async_copy(src, dst, load_sem.at[len(loads)])
        copy.start()
        loads.append(copy)

    load(w_out, wo)
    mine, theirs = pl.multiple_of(core * half, LANES), pl.multiple_of((1 - core) * half, LANES)
    deep = pl.ds(pl.multiple_of(core * depth, depth), depth)
    load(w_gate.at[:, pl.ds(mine, half)], wgu.at[deep, pl.ds(0, half)])
    load(w_up.at[:, pl.ds(mine, half)], wgu.at[deep, pl.ds(half, half)])
    load(w_down, wd)

    barrier = pltpu.get_barrier_semaphore()
    for device in (along_x.prev, along_x.follow, along_x.pair, along_z.prev, along_z.follow, along_z.pair, sib):
        pl.semaphore_signal(barrier, inc=1, device_id=device, device_id_type=MESH)
    pl.semaphore_wait(barrier, 7)

    gather_a = Gather(along_z, lambda k, c, b: attn_all.at[k, b, c], ga_send, ga_recv)
    gather_b = Gather(along_x, lambda k, c, b: normed_all.at[k, c, b], gb_send, gb_recv)
    gather_c = Gather(along_z, lambda k, c, b: hidden_all.at[k, c, b], gc_send, gc_recv)
    scatter_a = Scatter(along_x, lambda k: proj.at[k], far_a, near_a, last_a, sa_send, sa_recv)
    scatter_b = Scatter(along_z, lambda k: sums.at[k % 2], far_b, near_b, last_b, sb_send, sb_recv)
    scatter_c = Scatter(along_x, lambda k: proj.at[k], far_c, near_c, last_c, sc_send, sc_recv)

    swaps = [
        remote(
            w.at[:, pl.ds(theirs, half)],
            wgu.at[deep, pl.ds(n * half, half)],
            swap_send.at[n],
            swap_recv.at[n],
            sib,
        )
        for n, w in enumerate((w_gate, w_up))
    ]

    visible[...] = visible_nodes(parents[...], tree_size[0])

    def start(k):
        nodes = slice(k * NODES, (k + 1) * NODES)
        node = lax.broadcasted_iota(jnp.int32, (NODES, 1), 0) + k * NODES
        attn_all[k, along_z.block(yl, 0), core] = attend(
            queries[nodes, :], visible[nodes, :], node < tree_size[0], cache_len[0], tree_kv[...], cache, page_table
        )
        gather_a.step1(k)

    def project(k):
        gather_a.step5(k)
        if k == 0:
            loads[0].wait()

        def tile(n, carry):
            columns = pl.ds(pl.multiple_of(n * TILE, TILE), TILE)
            rows = attn_all[k].reshape(ROWS, attn_all.shape[-1])
            product = jnp.dot(rows, wo[:, columns], preferred_element_type=F32)
            proj[k, :, :, columns] = product.astype(BF).reshape(8, BLOCK, TILE)
            return carry

        lax.fori_loop(0, width // TILE, tile, 0)
        scatter_a.step1(k)
        if k == 0:
            for copy in swaps:
                copy.start()

    def norm(k):
        projected = scatter_a.step4(k)
        rows = jnp.concatenate([resid[r * MAXTREE + k * NODES : r * MAXTREE + (k + 1) * NODES, :] for r in (0, 1)], axis=0)
        value = (rows.astype(F32) + projected).astype(BF)
        hid[k] = value
        wide = value.astype(F32)
        mine = along_x.block(yh, 0)
        normed_all[k, core, mine, :, 0:width] = (wide * gain[...].astype(F32)).astype(BF)
        squares = jnp.sum(wide * wide, axis=1, keepdims=True)
        normed_all[k, core, mine, :, width:] = jnp.broadcast_to(squares, (BLOCK, LANES)).astype(BF)
        gather_b.step1(k)

    def gate_up(k):
        gather_b.step5(k)
        if k == 0:
            loads[1].wait()
            loads[2].wait()
            for copy in swaps:
                copy.wait()
        if k >= 2:
            scatter_b.close(k - 2)
        part = sums.at[k % 2]

        def tile(n, carry):
            columns = pl.ds(pl.multiple_of(n * TILE, TILE), TILE)
            product = jnp.dot(
                normed_all[k, 0, :, :, 0:width].reshape(ROWS, width), wgu[0:depth, columns], preferred_element_type=F32
            )
            product += jnp.dot(
                normed_all[k, 1, :, :, 0:width].reshape(ROWS, width), wgu[depth:, columns], preferred_element_type=F32
            )
            part[:, :, columns] = product.astype(BF).reshape(8, BLOCK, TILE)
            return carry

        lax.fori_loop(0, 2 * half // TILE, tile, 0)
        squares = normed_all[k, 0, :, :, width:].astype(F32) + normed_all[k, 1, :, :, width:].astype(F32)
        part[:, :, 2 * half :] = squares.astype(BF)
        scatter_b.step1(k)

    def activate(k):
        total = scatter_b.step4(k)
        scale = lax.rsqrt(total[:, 2 * half : 2 * half + 1] / D + EPSILON)
        gate = total[:, 0:half] * scale
        up = total[:, half : 2 * half] * scale
        hidden_all[k, core, along_z.block(yl, 0)] = (gate / (1.0 + jnp.exp(-gate)) * up).astype(BF)
        gather_c.step1(k)

    def down(k):
        gather_c.step5(k)
        if k == 0:
            loads[3].wait()
        scatter_a.close(k)

        def tile(n, carry):
            columns = pl.ds(pl.multiple_of(n * TILE, TILE), TILE)
            product = jnp.dot(
                hidden_all[k, 0].reshape(ROWS, half), wd[0:half, columns], preferred_element_type=F32
            )
            product += jnp.dot(
                hidden_all[k, 1].reshape(ROWS, half), wd[half:, columns], preferred_element_type=F32
            )
            proj[k, :, :, columns] = product.astype(BF).reshape(8, BLOCK, TILE)
            return carry

        lax.fori_loop(0, width // TILE, tile, 0)
        scatter_c.step1(k)

    def finish(k):
        total = (hid[k].astype(F32) + scatter_c.step4(k)).astype(BF)
        for r in (0, 1):
            out[r * MAXTREE + k * NODES : r * MAXTREE + (k + 1) * NODES, :] = total[r * NODES : (r + 1) * NODES, :]

    stages = [
        start,
        gather_a.step2,
        gather_a.step3,
        gather_a.step4,
        project,
        scatter_a.step2,
        scatter_a.step3,
        norm,
        gather_b.step2,
        gather_b.step3,
        gather_b.step4,
        gate_up,
        scatter_b.step2,
        scatter_b.step3,
        activate,
        gather_c.step2,
        gather_c.step3,
        gather_c.step4,
        down,
        scatter_c.step2,
        scatter_c.step3,
        finish,
    ]
    assert len(ORDER) == len(stages) * CHUNKS
    for stage, k in ORDER:
        stages[stage](k)
    for group in (gather_a, gather_b, gather_c, scatter_a, scatter_b, scatter_c):
        for k in range(CHUNKS):
            group.close(k)


ORDER = sorted(((s, k) for s in range(22) for k in range(CHUNKS)), key=lambda e: (e[0] + 2 * e[1], -e[1]))


def layer(page_table, cache_len, tree_size, parents, queries, tree_kv, cache, resid, gain, w_out, w_gate, w_up, w_down):
    heads, width = w_out.shape
    depth, units = w_gate.shape
    half = units // 2
    sums = 2 * half + LANES
    vmem = pl.BlockSpec(memory_space=pltpu.VMEM)
    smem = pl.BlockSpec(memory_space=pltpu.SMEM)
    hbm = pl.BlockSpec(memory_space=pl.ANY)
    sem = pltpu.SemaphoreType.DMA

    def scatter_buffers(lanes):
        return [
            pltpu.VMEM((CHUNKS, 2, BLOCK, lanes), BF),
            pltpu.VMEM((CHUNKS, 2, 2, BLOCK, lanes), BF),
            pltpu.VMEM((CHUNKS, BLOCK, lanes), BF),
        ]

    scratch = [
        pltpu.VMEM((heads, width), BF),
        pltpu.VMEM((2 * depth, units), BF),
        pltpu.VMEM((units, width), BF),
        pltpu.VMEM((CHUNKS, 8, 2, NODES, heads), BF),
        pltpu.VMEM((CHUNKS, 8, BLOCK, width), BF),
        pltpu.VMEM((CHUNKS, BLOCK, width), BF),
        pltpu.VMEM((CHUNKS, 2, 8, BLOCK, width + LANES), BF),
        pltpu.VMEM((2, 8, BLOCK, sums), BF),
        pltpu.VMEM((CHUNKS, 2, 8, BLOCK, half), BF),
        pltpu.VMEM((MAXTREE, MAXTREE), F32),
        *scatter_buffers(width),
        *scatter_buffers(sums),
        *scatter_buffers(width),
        sem((4,)),
        sem((2,)),
        sem((2,)),
        *[sem((CHUNKS, 15))] * 6,
        *[sem((CHUNKS, 7))] * 6,
    ]
    return pl.pallas_call(
        layer_kernel,
        out_shape=jax.ShapeDtypeStruct(resid.shape, BF),
        in_specs=[smem, smem, smem, vmem, vmem, vmem, vmem, vmem, vmem, hbm, hbm, hbm, hbm],
        out_specs=vmem,
        scratch_shapes=scratch,
        compiler_params=pltpu.CompilerParams(
            collective_id=0, has_side_effects=True, vmem_limit_bytes=62 * 1024 * 1024
        ),
        cost_estimate=pl.CostEstimate(
            flops=2 * 1024 * (heads * width + 3 * depth * units), bytes_accessed=26 * 1024 * 1024, transcendentals=0
        ),
    )(
        page_table,
        cache_len,
        tree_size,
        parents,
        queries,
        tree_kv,
        cache,
        resid,
        gain,
        w_out,
        w_gate,
        w_up,
        w_down,
    )


def body(
    resid,
    queries,
    tree_kv,
    cache,
    page_table,
    cache_len,
    tree_size,
    parents,
    w_out,
    gain,
    w_gate,
    w_up,
    w_down,
):
    return layer(
        page_table,
        cache_len,
        tree_size,
        parents,
        queries,
        tree_kv,
        cache,
        resid,
        gain.reshape(1, -1),
        w_out,
        w_gate,
        w_up,
        w_down,
    )


def solution(mesh):
    in_specs = (
        P("gx", "gy"),
        P("gy", "gx"),
        P("gy", "gx"),
        P("gx", "gy", None, None),
        P("gy", None),
        P("gy"),
        P("gy"),
        P("gy", None),
        P("gx", "gy"),
        P("gy"),
        P("gy", "gx"),
        P("gy", "gx"),
        P("gx", "gy"),
    )
    out_specs = P("gx", "gy")
    return jax.shard_map(body, mesh=mesh, in_specs=in_specs, out_specs=out_specs, check_vma=False)
```

time: 557 us -> 178 us (0.32)
  waiting for transfers between devices: 437 us -> 0 us
  Pallas kernels: 0 us -> 174 us
  matrix products: 52.3 us -> 0 us
  blocking collectives: 28 us -> 0 us
  other arithmetic: 21.4 us -> 0 us
  between operations: 15 us -> 1.31 us
    reduce_scatter x3 -> x0, waiting for transfers between devices: 302 us -> none  [the longest x1 150 us: body(): lax.psum_scatter(partial_units.astype(jnp.bfloat16), 'gy', scatter_dimens...]
    pallas_call x0 -> x1, Pallas kernels: none -> 174 us  [layer(): pl.pallas_call(layer_kernel, out_shape=jax.ShapeDtypeStruct(resid.shape,...]
    all_gather x3 -> x0, waiting for transfers between devices: 135 us -> none  [the longest x1 51.6 us: body(): shard_rows = lax.all_gather(normed, 'gx', axis=0, tiled=True)]
    dot_general x14 -> x0, matrix products: 52.3 us -> none  [the longest x1 12.5 us: body(): jnp.dot(rows, w_down, preferred_element_type=jnp.float32)]
    psum x1 -> x0, blocking collectives: 28 us -> none  [body(): square_total = lax.psum(jnp.sum(hid_wide * hid_wide, axis=1), 'gy')]
    concatenate x1 -> x0, other arithmetic: 8.96 us -> none  [body(): partial_units = jnp.concatenate([gate_part, up_part], axis=1)]
    convert_element_type x6 -> x0, other arithmetic: 6.17 us -> none  [the longest x1 1.78 us: body(): return (hid_wide + down).astype(jnp.bfloat16)]
  transfers between devices with their start and end apart: 6 -> 0, of which waited for: 6 -> 0; matrix products, arithmetic and copies ran while one was open for 0% -> 0% of each run, Pallas kernels for 0% -> 0%
where the time goes in v1:
time: 178 us
  Pallas kernels  174 us (98%)
  local copies, waits for them, and re-layouts  2.95 us (2%)
    pallas_call x1, Pallas kernels, layer(): pl.pallas_call(layer_kernel, out_shape=jax.ShapeDtypeStruct(resid.shape,...  174 us

profile of v1, /device:TPU:0, one launch (start us, length us, event | category | flops | bytes accessed | tf_op | source)
XLA Modules:
  0.0 178.2 jit_solution(16857182038899552904)
XLA Ops:
  1.3 1.3 reshape.3.gain
  2.6 173.9 %shard_map.127 = bf16[128,1024]{1,0:T(8,128)(2,1)} custom-call(s32[1,8]{1,0:T(1,128)} %page_table.1, s32[1]{0:T(128)S(6)} %copy.15.cache_len, s32[1]{0:T(128)S(6)} %copy.16.tree_size, s32[1,64]{1,0:T(1,128)} %parents.1, bf16[64,2048]{1,0:T(8,128)(2,1)} %queries.1, bf16[64,256]{1,0:T(8,128)(2,1)} %tree_kv.1, bf16[1,8,128,256]{3,2,1,0:T(8,128)(2,1)} %cache.1, ...), custom_call_target="tpu_custom_call" | custom-call | flops 25232932864 | bytes 27262976 | tf_op jit(solution)/shard_map/pallas_call | solution.py:509
  176.5 1.7 copy.17

commit v2 on v1

--- a/solution.py
+++ b/solution.py
@@ -21,7 +21,7 @@
 BLOCK = 2 * NODES
 ROWS = 8 * BLOCK
 LANES = 128
-TILE = 256
+TILE = 512
 
 
 def visible_nodes(parents, tree_len):
@@ -80,6 +80,22 @@
         device_id=device,
         device_id_type=MESH,
     )
+
+
+def multiply(rows, weights, result):
+    width = weights.shape[1]
+
+    def columns(at, size):
+        product = jnp.dot(rows(), weights[:, pl.ds(at, size)], preferred_element_type=F32)
+        result[:, :, pl.ds(at, size)] = product.astype(BF).reshape(8, BLOCK, size)
+
+    def tile(n, carry):
+        columns(pl.multiple_of(n * TILE, TILE), TILE)
+        return carry
+
+    lax.fori_loop(0, width // TILE, tile, 0)
+    if width % TILE:
+        columns(width - width % TILE, width % TILE)
 
 
 class Place:
@@ -349,14 +365,7 @@
         if k == 0:
             loads[0].wait()
 
-        def tile(n, carry):
-            columns = pl.ds(pl.multiple_of(n * TILE, TILE), TILE)
-            rows = attn_all[k].reshape(ROWS, attn_all.shape[-1])
-            product = jnp.dot(rows, wo[:, columns], preferred_element_type=F32)
-            proj[k, :, :, columns] = product.astype(BF).reshape(8, BLOCK, TILE)
-            return carry
-
-        lax.fori_loop(0, width // TILE, tile, 0)
+        multiply(lambda: attn_all[k].reshape(ROWS, attn_all.shape[-1]), wo, proj.at[k])
         scatter_a.step1(k)
         if k == 0:
             for copy in swaps:
@@ -369,7 +378,7 @@
         hid[k] = value
         wide = value.astype(F32)
         mine = along_x.block(yh, 0)
-        normed_all[k, core, mine, :, 0:width] = (wide * gain[...].astype(F32)).astype(BF)
+        normed_all[k, core, mine, :, 0:width] = (wide * gain[...].astype(F32).reshape(1, width)).astype(BF)
         squares = jnp.sum(wide * wide, axis=1, keepdims=True)
         normed_all[k, core, mine, :, width:] = jnp.broadcast_to(squares, (BLOCK, LANES)).astype(BF)
         gather_b.step1(k)
@@ -385,18 +394,13 @@
             scatter_b.close(k - 2)
         part = sums.at[k % 2]
 
-        def tile(n, carry):
-            columns = pl.ds(pl.multiple_of(n * TILE, TILE), TILE)
-            product = jnp.dot(
-                normed_all[k, 0, :, :, 0:width].reshape(ROWS, width), wgu[0:depth, columns], preferred_element_type=F32
-            )
-            product += jnp.dot(
-                normed_all[k, 1, :, :, 0:width].reshape(ROWS, width), wgu[depth:, columns], preferred_element_type=F32
-            )
-            part[:, :, columns] = product.astype(BF).reshape(8, BLOCK, TILE)
-            return carry
-
-        lax.fori_loop(0, 2 * half // TILE, tile, 0)
+        multiply(
+            lambda: jnp.concatenate(
+                [normed_all[k, c, :, :, 0:width].reshape(ROWS, width) for c in (0, 1)], axis=1
+            ),
+            wgu,
+            part,
+        )
         squares = normed_all[k, 0, :, :, width:].astype(F32) + normed_all[k, 1, :, :, width:].astype(F32)
         part[:, :, 2 * half :] = squares.astype(BF)
         scatter_b.step1(k)
@@ -415,18 +419,9 @@
             loads[3].wait()
         scatter_a.close(k)
 
-        def tile(n, carry):
-            columns = pl.ds(pl.multiple_of(n * TILE, TILE), TILE)
-            product = jnp.dot(
-                hidden_all[k, 0].reshape(ROWS, half), wd[0:half, columns], preferred_element_type=F32
-            )
-            product += jnp.dot(
-                hidden_all[k, 1].reshape(ROWS, half), wd[half:, columns], preferred_element_type=F32
-            )
-            proj[k, :, :, columns] = product.astype(BF).reshape(8, BLOCK, TILE)
-            return carry
-
-        lax.fori_loop(0, width // TILE, tile, 0)
+        multiply(
+            lambda: jnp.concatenate([hidden_all[k, c].reshape(ROWS, half) for c in (0, 1)], axis=1), wd, proj.at[k]
+        )
         scatter_c.step1(k)
 
     def finish(k):
@@ -458,15 +453,20 @@
         scatter_c.step3,
         finish,
     ]
-    assert len(ORDER) == len(stages) * CHUNKS
-    for stage, k in ORDER:
-        stages[stage](k)
+    ahead = [iter(stages) for k in range(CHUNKS)]
+    for k in TURNS:
+        next(ahead[k])(k)
     for group in (gather_a, gather_b, gather_c, scatter_a, scatter_b, scatter_c):
         for k in range(CHUNKS):
             group.close(k)
 
 
-ORDER = sorted(((s, k) for s in range(22) for k in range(CHUNKS)), key=lambda e: (e[0] + 2 * e[1], -e[1]))
+TURNS = (
+    0, 1, 0, 3, 0, 1, 2, 0, 1, 0, 2, 0, 1, 2, 0, 1, 2, 3, 0, 1, 2, 3,
+    1, 0, 3, 2, 0, 1, 2, 3, 0, 1, 0, 1, 2, 3, 1, 2, 0, 3, 1, 0, 2, 2,
+    3, 1, 0, 2, 3, 1, 3, 0, 3, 1, 2, 0, 3, 0, 2, 0, 3, 1, 2, 0, 2, 3,
+    1, 2, 3, 1, 0, 2, 3, 1, 3, 2, 3, 1, 2, 3, 1, 2, 0, 3, 3, 2, 1, 3,
+)
 
 
 def layer(page_table, cache_len, tree_size, parents, queries, tree_kv, cache, resid, gain, w_out, w_gate, w_up, w_down):
@@ -559,7 +559,7 @@
         tree_kv,
         cache,
         resid,
-        gain.reshape(1, -1),
+        gain,
         w_out,
         w_gate,
         w_up,

time: 178 us -> 171 us (0.961)
  Pallas kernels: 174 us -> 168 us
    pallas_call x1, Pallas kernels: 174 us -> 168 us  [layer(): pl.pallas_call(layer_kernel, out_shape=jax.ShapeDtypeStruct(resid.shape,...]
where the time goes in v2:
time: 171 us
  Pallas kernels  168 us (98%)
    pallas_call x1, Pallas kernels, layer(): pl.pallas_call(layer_kernel, out_shape=jax.ShapeDtypeStruct(resid.shape,...  168 us

profile of v2, /device:TPU:0, one launch (start us, length us, event | category | flops | bytes accessed | tf_op | source)
XLA Modules:
  0.0 170.6 jit_solution(14006189948073318514)
XLA Ops:
  1.3 167.7 %shard_map.127 = bf16[128,1024]{1,0:T(8,128)(2,1)} custom-call(s32[1,8]{1,0:T(1,128)} %page_table.1, s32[1]{0:T(128)S(6)} %copy.15.cache_len, s32[1]{0:T(128)S(6)} %copy.16.tree_size, s32[1,64]{1,0:T(1,128)} %parents.1, bf16[64,2048]{1,0:T(8,128)(2,1)} %queries.1, bf16[64,256]{1,0:T(8,128)(2,1)} %tree_kv.1, bf16[1,8,128,256]{3,2,1,0:T(8,128)(2,1)} %cache.1, ...), custom_call_target="tpu_custom_call" | custom-call | flops 25232932864 | bytes 27262976 | tf_op jit(solution)/shard_map/pallas_call | solution.py:509
  169.0 1.7 copy.17

commit v3 on v2

--- a/solution.py
+++ b/solution.py
@@ -21,7 +21,7 @@
 BLOCK = 2 * NODES
 ROWS = 8 * BLOCK
 LANES = 128
-TILE = 512
+TILE = 1024
 
 
 def visible_nodes(parents, tree_len):
@@ -182,8 +182,11 @@
         ref = self.ref(k, core, block)
         remote(ref, ref, self.send.at[k, sem], self.recv.at[k, sem], self.at.pair).wait_recv()
 
-    def share(self, k, block):
-        self.push(k, block, 7 + block, self.at.sib)
+    def both(self, shift):
+        return pl.ds(self.at.block(0, shift), 2)
+
+    def share(self, k, shift):
+        self.push(k, self.both(shift), 7 + shift % 4, self.at.sib)
 
     def step1(self, k):
         at = self.at
@@ -191,7 +194,6 @@
         self.push(k, mine, 0, at.pair)
         self.push(k, mine, 1 + at.p, at.follow)
         self.push(k, mine, 3 + at.p, at.prev)
-        self.share(k, mine)
 
     def step2(self, k):
         at = self.at
@@ -200,34 +202,29 @@
         self.arrived(k, block, 0, at.core)
         self.push(k, block, 1 + other, at.follow)
         self.push(k, block, 3 + other, at.prev)
-        self.share(k, block)
+        self.share(k, 0)
 
     def step3(self, k):
         at = self.at
         left, right = at.block(0, -1), at.block(1, 1)
         self.arrived(k, left, 1, at.core)
         self.push(k, left, 5, at.follow)
-        self.share(k, left)
         self.arrived(k, right, 4, at.core)
         self.push(k, right, 6, at.prev)
-        self.share(k, right)
-        left, right = at.block(1, -1), at.block(0, 1)
-        self.arrived(k, left, 2, at.core)
-        self.share(k, left)
-        self.arrived(k, right, 3, at.core)
-        self.share(k, right)
+        self.arrived(k, at.block(1, -1), 2, at.core)
+        self.share(k, -1)
+        self.arrived(k, at.block(0, 1), 3, at.core)
+        self.share(k, 1)
 
     def step4(self, k):
         at = self.at
-        left, right = at.block(0, -2), at.block(1, 2)
-        self.arrived(k, left, 5, at.core)
-        self.share(k, left)
-        self.arrived(k, right, 6, at.core)
-        self.share(k, right)
+        self.arrived(k, at.block(0, 2), 5, at.core)
+        self.arrived(k, at.block(1, 2), 6, at.core)
+        self.share(k, 2)
 
     def step5(self, k):
-        for block in range(8):
-            self.arrived(k, block, 7 + block, 1 - self.at.core)
+        for shift in (0, 1, -1, 2):
+            self.arrived(k, self.both(shift), 7 + shift % 4, 1 - self.at.core)
 
     def close(self, k):
         for copy in self.open.pop(k, []):
@@ -300,7 +297,7 @@
         ((1 - yh) * 4 + x, gy),
         sib,
         core,
-        lambda p, r: p * 4 + r,
+        lambda p, r: r * 2 + p,
     )
     along_z = Place(
         z,
@@ -365,7 +362,13 @@
         if k == 0:
             loads[0].wait()
 
-        multiply(lambda: attn_all[k].reshape(ROWS, attn_all.shape[-1]), wo, proj.at[k])
+        multiply(
+            lambda: jnp.concatenate(
+                [attn_all[k, q].reshape(BLOCK, attn_all.shape[-1]) for q in (0, 4, 1, 5, 2, 6, 3, 7)], axis=0
+            ),
+            wo,
+            proj.at[k],
+        )
         scatter_a.step1(k)
         if k == 0:
             for copy in swaps:
@@ -462,10 +465,10 @@
 
 
 TURNS = (
-    0, 1, 0, 3, 0, 1, 2, 0, 1, 0, 2, 0, 1, 2, 0, 1, 2, 3, 0, 1, 2, 3,
-    1, 0, 3, 2, 0, 1, 2, 3, 0, 1, 0, 1, 2, 3, 1, 2, 0, 3, 1, 0, 2, 2,
-    3, 1, 0, 2, 3, 1, 3, 0, 3, 1, 2, 0, 3, 0, 2, 0, 3, 1, 2, 0, 2, 3,
-    1, 2, 3, 1, 0, 2, 3, 1, 3, 2, 3, 1, 2, 3, 1, 2, 0, 3, 3, 2, 1, 3,
+    0, 1, 0, 3, 0, 1, 2, 0, 1, 0, 2, 1, 0, 1, 2, 3, 0, 1, 2, 3, 0, 2,
+    1, 3, 0, 2, 0, 1, 3, 0, 2, 1, 0, 1, 2, 3, 1, 2, 0, 3, 1, 2, 0, 3,
+    2, 1, 0, 2, 1, 3, 3, 0, 3, 1, 2, 0, 3, 2, 0, 3, 0, 2, 1, 3, 2, 1,
+    0, 2, 3, 1, 0, 2, 3, 1, 3, 2, 1, 3, 2, 3, 1, 3, 2, 0, 3, 2, 1, 3,
 )
 
 
@@ -503,7 +506,7 @@
         sem((4,)),
         sem((2,)),
         sem((2,)),
-        *[sem((CHUNKS, 15))] * 6,
+        *[sem((CHUNKS, 11))] * 6,
         *[sem((CHUNKS, 7))] * 6,
     ]
     return pl.pallas_call(

time: 171 us -> 168 us (0.982)
  Pallas kernels: 168 us -> 163 us
    pallas_call x1, Pallas kernels: 168 us -> 163 us  [layer(): pl.pallas_call(layer_kernel, out_shape=jax.ShapeDtypeStruct(resid.shape,...]
where the time goes in v3:
time: 168 us; the launch traced here: 166 us
  Pallas kernels  163 us (97%)
    pallas_call x1, Pallas kernels, layer(): pl.pallas_call(layer_kernel, out_shape=jax.ShapeDtypeStruct(resid.shape,...  163 us

profile of v3, /device:TPU:0, one launch (start us, length us, event | category | flops | bytes accessed | tf_op | source)
XLA Modules:
  0.0 166.4 jit_solution(6013694235634379074)
XLA Ops:
  1.3 163.4 %shard_map.127 = bf16[128,1024]{1,0:T(8,128)(2,1)} custom-call(s32[1,8]{1,0:T(1,128)} %page_table.1, s32[1]{0:T(128)S(6)} %copy.15.cache_len, s32[1]{0:T(128)S(6)} %copy.16.tree_size, s32[1,64]{1,0:T(1,128)} %parents.1, bf16[64,2048]{1,0:T(8,128)(2,1)} %queries.1, bf16[64,256]{1,0:T(8,128)(2,1)} %tree_kv.1, bf16[1,8,128,256]{3,2,1,0:T(8,128)(2,1)} %cache.1, ...), custom_call_target="tpu_custom_call" | custom-call | flops 25232932864 | bytes 27262976 | tf_op jit(solution)/shard_map/pallas_call | solution.py:512
  164.7 1.7 %copy.17 = bf16[128,1024]{1,0:T(8,128)(2,1)} copy(bf16[128,1024]{1,0:T(8,128)(2,1)} %shard_map.127) | data formatting | bytes 524288

commit v4 on v3

--- a/solution.py
+++ b/solution.py
@@ -21,6 +21,7 @@
 BLOCK = 2 * NODES
 ROWS = 8 * BLOCK
 LANES = 128
+FRONT, BACK = pl.ds(0, BLOCK // 2), pl.ds(BLOCK // 2, BLOCK // 2)
 TILE = 1024
 
 
@@ -109,10 +110,10 @@
         return self.index(p, lax.rem(self.r + (4 + shift), 4))
 
 
-class Scatter:
-    def __init__(self, place, part, far, near, last, send, recv):
+class PairScatter:
+    def __init__(self, place, part, first, far, near, last, send, recv):
         self.at = place
-        self.part, self.far, self.near, self.last = part, far, near, last
+        self.part, self.first, self.far, self.near, self.last = part, first, far, near, last
         self.send, self.recv = send, recv
         self.open = {}
 
@@ -126,25 +127,24 @@
 
     def step1(self, k):
         at, part = self.at, self.part(k)
-        self.push(k, part.at[at.block(0, 2)], self.far.at[k, 0], 0, at.follow)
-        self.push(k, part.at[at.block(1, 2)], self.far.at[k, 1], 1, at.prev)
-        self.push(k, part.at[at.block(1, 1)], self.near.at[k, 0, 1], 3, at.follow)
-        self.push(k, part.at[at.block(0, -1)], self.near.at[k, 1, 0], 4, at.prev)
+        p, other = at.p, 1 - at.p
+        self.push(k, part.at[at.block(other, 2)], self.first.at[k], 0, at.pair)
+        self.push(k, part.at[at.block(other, 1)], self.near.at[k, 0, other], 3, at.follow)
+        self.push(k, part.at[at.block(other, -1)], self.near.at[k, 1, other], 4, at.prev)
+        self.push(k, part.at[at.block(p, 1), BACK], self.near.at[k, 0, p, BACK], 6, at.follow)
+        self.push(k, part.at[at.block(p, -1), FRONT], self.near.at[k, 1, p, FRONT], 8, at.prev)
 
     def step2(self, k):
         at, part = self.at, self.part(k)
-        for way, (p, shift, device, sem) in enumerate(((0, 1, at.follow, 2), (1, -1, at.prev, 5))):
-            self.arrived(k, self.far.at[k, way], way)
-            mine = at.block(p, shift)
-            part[mine] = (part[mine].astype(F32) + self.far[k, way].astype(F32)).astype(BF)
-            self.push(k, part.at[mine], self.near.at[k, way, p], sem, device)
+        self.arrived(k, self.first.at[k], 0)
+        mine = at.block(at.p, 2)
+        part[mine] = (part[mine].astype(F32) + self.first[k].astype(F32)).astype(BF)
+        self.push(k, part.at[mine, FRONT], self.far.at[k, 0], 1, at.follow)
+        self.push(k, part.at[mine, BACK], self.far.at[k, 1], 2, at.prev)
 
     def ring_sum(self, k, p):
-        part = self.part(k)
-        for way in (0, 1):
-            self.arrived(k, self.near.at[k, way, p], 2 + 2 * way + p)
         return (
-            part[self.at.block(p, 0)].astype(F32)
+            self.part(k)[self.at.block(p, 0)].astype(F32)
             + self.near[k, 0, p].astype(F32)
             + self.near[k, 1, p].astype(F32)
         )
@@ -152,14 +152,27 @@
     def step3(self, k):
         at, part = self.at, self.part(k)
         other = 1 - at.p
+        self.arrived(k, self.near.at[k, 0, other], 3)
+        self.arrived(k, self.near.at[k, 1, other], 4)
         theirs = at.block(other, 0)
         part[theirs] = self.ring_sum(k, other).astype(BF)
-        self.push(k, part.at[theirs], self.last.at[k], 6, at.pair)
+        self.push(k, part.at[theirs], self.last.at[k], 9, at.pair)
 
     def step4(self, k):
-        total = self.ring_sum(k, self.at.p)
-        self.arrived(k, self.last.at[k], 6)
-        return total + self.last[k].astype(F32)
+        at, part = self.at, self.part(k)
+        for way, (shift, rows, sem, device) in enumerate(((1, FRONT, 5, at.follow), (-1, BACK, 7, at.prev))):
+            self.arrived(k, self.far.at[k, way], 1 + way)
+            mine = at.block(at.p, shift)
+            part[mine, rows] = (part[mine, rows].astype(F32) + self.far[k, way].astype(F32)).astype(BF)
+            self.push(k, part.at[mine, rows], self.near.at[k, way, at.p, rows], sem, device)
+
+    def step5(self, k):
+        p = self.at.p
+        for way, (added, alone) in enumerate(((FRONT, BACK), (BACK, FRONT))):
+            self.arrived(k, self.near.at[k, way, p, added], 5 + 2 * way)
+            self.arrived(k, self.near.at[k, way, p, alone], 6 + 2 * way)
+        self.arrived(k, self.last.at[k], 9)
+        return self.ring_sum(k, p) + self.last[k].astype(F32)
 
     def close(self, k):
         for copy in self.open.pop(k, []):
@@ -256,12 +269,15 @@
     sums,
     hidden_all,
     visible,
+    first_a,
     far_a,
     near_a,
     last_a,
+    first_b,
     far_b,
     near_b,
     last_b,
+    first_c,
     far_c,
     near_c,
     last_c,
@@ -332,9 +348,9 @@
     gather_a = Gather(along_z, lambda k, c, b: attn_all.at[k, b, c], ga_send, ga_recv)
     gather_b = Gather(along_x, lambda k, c, b: normed_all.at[k, c, b], gb_send, gb_recv)
     gather_c = Gather(along_z, lambda k, c, b: hidden_all.at[k, c, b], gc_send, gc_recv)
-    scatter_a = Scatter(along_x, lambda k: proj.at[k], far_a, near_a, last_a, sa_send, sa_recv)
-    scatter_b = Scatter(along_z, lambda k: sums.at[k % 2], far_b, near_b, last_b, sb_send, sb_recv)
-    scatter_c = Scatter(along_x, lambda k: proj.at[k], far_c, near_c, last_c, sc_send, sc_recv)
+    scatter_a = PairScatter(along_x, lambda k: proj.at[k], first_a, far_a, near_a, last_a, sa_send, sa_recv)
+    scatter_b = PairScatter(along_z, lambda k: sums.at[k % 2], first_b, far_b, near_b, last_b, sb_send, sb_recv)
+    scatter_c = PairScatter(along_x, lambda k: proj.at[k], first_c, far_c, near_c, last_c, sc_send, sc_recv)
 
     swaps = [
         remote(
@@ -375,7 +391,7 @@
                 copy.start()
 
     def norm(k):
-        projected = scatter_a.step4(k)
+        projected = scatter_a.step5(k)
         rows = jnp.concatenate([resid[r * MAXTREE + k * NODES : r * MAXTREE + (k + 1) * NODES, :] for r in (0, 1)], axis=0)
         value = (rows.astype(F32) + projected).astype(BF)
         hid[k] = value
@@ -409,7 +425,7 @@
         scatter_b.step1(k)
 
     def activate(k):
-        total = scatter_b.step4(k)
+        total = scatter_b.step5(k)
         scale = lax.rsqrt(total[:, 2 * half : 2 * half + 1] / D + EPSILON)
         gate = total[:, 0:half] * scale
         up = total[:, half : 2 * half] * scale
@@ -428,7 +444,7 @@
         scatter_c.step1(k)
 
     def finish(k):
-        total = (hid[k].astype(F32) + scatter_c.step4(k)).astype(BF)
+        total = (hid[k].astype(F32) + scatter_c.step5(k)).astype(BF)
         for r in (0, 1):
             out[r * MAXTREE + k * NODES : r * MAXTREE + (k + 1) * NODES, :] = total[r * NODES : (r + 1) * NODES, :]
 
@@ -440,6 +456,7 @@
         project,
         scatter_a.step2,
         scatter_a.step3,
+        scatter_a.step4,
         norm,
         gather_b.step2,
         gather_b.step3,
@@ -447,6 +464,7 @@
         gate_up,
         scatter_b.step2,
         scatter_b.step3,
+        scatter_b.step4,
         activate,
         gather_c.step2,
         gather_c.step3,
@@ -454,6 +472,7 @@
         down,
         scatter_c.step2,
         scatter_c.step3,
+        scatter_c.step4,
         finish,
     ]
     ahead = [iter(stages) for k in range(CHUNKS)]
@@ -465,10 +484,11 @@
 
 
 TURNS = (
-    0, 1, 0, 3, 0, 1, 2, 0, 1, 0, 2, 1, 0, 1, 2, 3, 0, 1, 2, 3, 0, 2,
-    1, 3, 0, 2, 0, 1, 3, 0, 2, 1, 0, 1, 2, 3, 1, 2, 0, 3, 1, 2, 0, 3,
-    2, 1, 0, 2, 1, 3, 3, 0, 3, 1, 2, 0, 3, 2, 0, 3, 0, 2, 1, 3, 2, 1,
-    0, 2, 3, 1, 0, 2, 3, 1, 3, 2, 1, 3, 2, 3, 1, 3, 2, 0, 3, 2, 1, 3,
+    0, 1, 0, 2, 0, 3, 0, 1, 2, 0, 3, 1, 2, 0, 0, 1, 0, 1, 0, 3, 1, 1,
+    2, 1, 0, 2, 3, 0, 1, 3, 2, 0, 2, 1, 0, 2, 1, 2, 3, 1, 0, 3, 2, 0,
+    3, 0, 1, 2, 0, 3, 2, 1, 2, 3, 1, 3, 1, 2, 0, 1, 3, 2, 2, 0, 1, 3,
+    1, 0, 0, 3, 2, 1, 3, 3, 2, 1, 2, 3, 1, 1, 0, 2, 3, 2, 3, 0, 2, 3,
+    2, 0, 3, 2, 0, 1, 3, 3, 3, 2, 1, 3,
 )
 
 
@@ -484,7 +504,8 @@
 
     def scatter_buffers(lanes):
         return [
-            pltpu.VMEM((CHUNKS, 2, BLOCK, lanes), BF),
+            pltpu.VMEM((CHUNKS, BLOCK, lanes), BF),
+            pltpu.VMEM((CHUNKS, 2, BLOCK // 2, lanes), BF),
             pltpu.VMEM((CHUNKS, 2, 2, BLOCK, lanes), BF),
             pltpu.VMEM((CHUNKS, BLOCK, lanes), BF),
         ]
@@ -507,7 +528,7 @@
         sem((2,)),
         sem((2,)),
         *[sem((CHUNKS, 11))] * 6,
-        *[sem((CHUNKS, 7))] * 6,
+        *[sem((CHUNKS, 10))] * 6,
     ]
     return pl.pallas_call(
         layer_kernel,

time: 168 us -> 165 us (0.982)
  Pallas kernels: 163 us -> 161 us
    pallas_call x1, Pallas kernels: 163 us -> 161 us  [layer(): pl.pallas_call(layer_kernel, out_shape=jax.ShapeDtypeStruct(resid.shape,...]
where the time goes in v4:
time: 165 us; the launch traced here: 164 us
  Pallas kernels  161 us (98%)
  local copies, waits for them, and re-layouts  1.67 us (1%)
    pallas_call x1, Pallas kernels, layer(): pl.pallas_call(layer_kernel, out_shape=jax.ShapeDtypeStruct(resid.shape,...  161 us

profile of v4, /device:TPU:0, one launch (start us, length us, event | category | flops | bytes accessed | tf_op | source)
XLA Modules:
  0.0 164.1 jit_solution(9400671219580305031)
XLA Ops:
  1.3 161.1 %shard_map.127 = bf16[128,1024]{1,0:T(8,128)(2,1)} custom-call(s32[1,8]{1,0:T(1,128)} %page_table.1, s32[1]{0:T(128)S(6)} %copy.15.cache_len, s32[1]{0:T(128)S(6)} %copy.16.tree_size, s32[1,64]{1,0:T(1,128)} %parents.1, bf16[64,2048]{1,0:T(8,128)(2,1)} %queries.1, bf16[64,256]{1,0:T(8,128)(2,1)} %tree_kv.1, bf16[1,8,128,256]{3,2,1,0:T(8,128)(2,1)} %cache.1, ...), custom_call_target="tpu_custom_call" | custom-call | flops 25232932864 | bytes 27262976 | tf_op jit(solution)/shard_map/pallas_call | solution.py:533
  162.4 1.7 %copy.17 = bf16[128,1024]{1,0:T(8,128)(2,1)} copy(bf16[128,1024]{1,0:T(8,128)(2,1)} %shard_map.127) | data formatting | bytes 524288

commit v5 on v3

--- a/solution.py
+++ b/solution.py
@@ -21,7 +21,9 @@
 BLOCK = 2 * NODES
 ROWS = 8 * BLOCK
 LANES = 128
+FRONT, BACK = pl.ds(0, BLOCK // 2), pl.ds(BLOCK // 2, BLOCK // 2)
 TILE = 1024
+PIECES = 4
 
 
 def visible_nodes(parents, tree_len):
@@ -82,20 +84,13 @@
     )
 
 
-def multiply(rows, weights, result):
+def multiply(rows, weights, result, tile, done):
     width = weights.shape[1]
-
-    def columns(at, size):
-        product = jnp.dot(rows(), weights[:, pl.ds(at, size)], preferred_element_type=F32)
-        result[:, :, pl.ds(at, size)] = product.astype(BF).reshape(8, BLOCK, size)
-
-    def tile(n, carry):
-        columns(pl.multiple_of(n * TILE, TILE), TILE)
-        return carry
-
-    lax.fori_loop(0, width // TILE, tile, 0)
-    if width % TILE:
-        columns(width - width % TILE, width % TILE)
+    for j, at in enumerate(range(0, width, tile)):
+        size = min(tile, width - at)
+        product = jnp.dot(rows(), weights[:, at : at + size], preferred_element_type=F32)
+        result[:, :, at : at + size] = product.astype(BF).reshape(8, BLOCK, size)
+        done(j)
 
 
 class Place:
@@ -110,60 +105,125 @@
 
 
 class Scatter:
-    def __init__(self, place, part, far, near, last, send, recv):
-        self.at = place
-        self.part, self.far, self.near, self.last = part, far, near, last
+    def __init__(self, place, part, buffers, send, recv, cuts):
+        self.at, self.part = place, part
+        self.far, self.near, self.last = buffers
         self.send, self.recv = send, recv
+        self.cuts = cuts
         self.open = {}
 
-    def push(self, k, src, dst, sem, device):
-        copy = remote(src, dst, self.send.at[k, sem], self.recv.at[k, sem], device)
+    def push(self, slot, src, dst, sem, device):
+        copy = remote(src, dst, self.send.at[slot, sem], self.recv.at[slot, sem], device)
         copy.start()
-        self.open.setdefault(k, []).append(copy)
-
-    def arrived(self, k, ref, sem):
-        remote(ref, ref, self.send.at[k, sem], self.recv.at[k, sem], self.at.pair).wait_recv()
-
-    def step1(self, k):
+        return copy
+
+    def hand(self, k, src, dst, sem, device):
+        self.open.setdefault(k, []).append(self.push(k * len(self.cuts), src, dst, sem, device))
+
+    def arrived(self, k, ref, sem, pieces=False):
+        for j, columns in enumerate(self.cuts if pieces else [None]):
+            slot = k * len(self.cuts) + j
+            piece = ref.at[:, columns] if pieces else ref
+            remote(piece, piece, self.send.at[slot, sem], self.recv.at[slot, sem], self.at.pair).wait_recv()
+
+    def first_sends(self, k):
         at, part = self.at, self.part(k)
-        self.push(k, part.at[at.block(0, 2)], self.far.at[k, 0], 0, at.follow)
-        self.push(k, part.at[at.block(1, 2)], self.far.at[k, 1], 1, at.prev)
-        self.push(k, part.at[at.block(1, 1)], self.near.at[k, 0, 1], 3, at.follow)
-        self.push(k, part.at[at.block(0, -1)], self.near.at[k, 1, 0], 4, at.prev)
+        return [
+            (part.at[at.block(0, 2)], self.far.at[k, 0], 0, at.follow),
+            (part.at[at.block(1, 2)], self.far.at[k, 1], 1, at.prev),
+            (part.at[at.block(1, 1)], self.near.at[k, 0, 1], 3, at.follow),
+            (part.at[at.block(0, -1)], self.near.at[k, 1, 0], 4, at.prev),
+        ]
+
+    def step1(self, k, j):
+        columns = self.cuts[j]
+        for src, dst, sem, device in self.first_sends(k):
+            copy = self.push(k * len(self.cuts) + j, src.at[:, columns], dst.at[:, columns], sem, device)
+            self.open.setdefault(k, []).append(copy)
 
     def step2(self, k):
         at, part = self.at, self.part(k)
         for way, (p, shift, device, sem) in enumerate(((0, 1, at.follow, 2), (1, -1, at.prev, 5))):
-            self.arrived(k, self.far.at[k, way], way)
+            self.arrived(k, self.far.at[k, way], way, True)
             mine = at.block(p, shift)
             part[mine] = (part[mine].astype(F32) + self.far[k, way].astype(F32)).astype(BF)
-            self.push(k, part.at[mine], self.near.at[k, way, p], sem, device)
+            self.hand(k, part.at[mine], self.near.at[k, way, p], sem, device)
 
     def ring_sum(self, k, p):
-        part = self.part(k)
-        for way in (0, 1):
-            self.arrived(k, self.near.at[k, way, p], 2 + 2 * way + p)
         return (
-            part[self.at.block(p, 0)].astype(F32)
+            self.part(k)[self.at.block(p, 0)].astype(F32)
             + self.near[k, 0, p].astype(F32)
             + self.near[k, 1, p].astype(F32)
         )
 
     def step3(self, k):
         at, part = self.at, self.part(k)
+        self.arrived(k, self.near.at[k, 0, 0], 2)
+        self.arrived(k, self.near.at[k, 0, 1], 3, True)
+        self.arrived(k, self.near.at[k, 1, 0], 4, True)
+        self.arrived(k, self.near.at[k, 1, 1], 5)
         other = 1 - at.p
         theirs = at.block(other, 0)
         part[theirs] = self.ring_sum(k, other).astype(BF)
-        self.push(k, part.at[theirs], self.last.at[k], 6, at.pair)
-
-    def step4(self, k):
-        total = self.ring_sum(k, self.at.p)
+        self.hand(k, part.at[theirs], self.last.at[k], 6, at.pair)
+
+    def total(self, k):
         self.arrived(k, self.last.at[k], 6)
-        return total + self.last[k].astype(F32)
+        return self.ring_sum(k, self.at.p) + self.last[k].astype(F32)
 
     def close(self, k):
         for copy in self.open.pop(k, []):
             copy.wait_send()
+
+
+class PairScatter(Scatter):
+    def __init__(self, place, part, buffers, send, recv, cuts):
+        super().__init__(place, part, buffers[1:], send, recv, cuts)
+        self.first = buffers[0]
+
+    def first_sends(self, k):
+        at, part = self.at, self.part(k)
+        p, other = at.p, 1 - at.p
+        return [
+            (part.at[at.block(other, 2)], self.first.at[k], 0, at.pair),
+            (part.at[at.block(other, 1)], self.near.at[k, 0, other], 3, at.follow),
+            (part.at[at.block(other, -1)], self.near.at[k, 1, other], 4, at.prev),
+            (part.at[at.block(p, 1), BACK], self.near.at[k, 0, p, BACK], 6, at.follow),
+            (part.at[at.block(p, -1), FRONT], self.near.at[k, 1, p, FRONT], 8, at.prev),
+        ]
+
+    def step2(self, k):
+        at, part = self.at, self.part(k)
+        self.arrived(k, self.first.at[k], 0, True)
+        mine = at.block(at.p, 2)
+        part[mine] = (part[mine].astype(F32) + self.first[k].astype(F32)).astype(BF)
+        self.hand(k, part.at[mine, FRONT], self.far.at[k, 0], 1, at.follow)
+        self.hand(k, part.at[mine, BACK], self.far.at[k, 1], 2, at.prev)
+
+    def step3(self, k):
+        at, part = self.at, self.part(k)
+        other = 1 - at.p
+        self.arrived(k, self.near.at[k, 0, other], 3, True)
+        self.arrived(k, self.near.at[k, 1, other], 4, True)
+        theirs = at.block(other, 0)
+        part[theirs] = self.ring_sum(k, other).astype(BF)
+        self.hand(k, part.at[theirs], self.last.at[k], 9, at.pair)
+
+    def step4(self, k):
+        at, part = self.at, self.part(k)
+        for way, (shift, rows, sem, device) in enumerate(((1, FRONT, 5, at.follow), (-1, BACK, 7, at.prev))):
+            self.arrived(k, self.far.at[k, way], 1 + way)
+            mine = at.block(at.p, shift)
+            part[mine, rows] = (part[mine, rows].astype(F32) + self.far[k, way].astype(F32)).astype(BF)
+            self.hand(k, part.at[mine, rows], self.near.at[k, way, at.p, rows], sem, device)
+
+    def total(self, k):
+        p = self.at.p
+        for way, (added, alone) in enumerate(((FRONT, BACK), (BACK, FRONT))):
+            self.arrived(k, self.near.at[k, way, p, added], 5 + 2 * way)
+            self.arrived(k, self.near.at[k, way, p, alone], 6 + 2 * way, True)
+        self.arrived(k, self.last.at[k], 9)
+        return self.ring_sum(k, p) + self.last[k].astype(F32)
 
 
 class Gather:
@@ -229,6 +289,58 @@
     def close(self, k):
         for copy in self.open.pop(k, []):
             copy.wait_send()
+
+
+class PairGather(Gather):
+    def hand(self, k, ref, sem, device):
+        copy = remote(ref, ref, self.send.at[k, sem], self.recv.at[k, sem], device)
+        copy.start()
+        self.open.setdefault(k, []).append(copy)
+
+    def landed(self, k, ref, sem):
+        remote(ref, ref, self.send.at[k, sem], self.recv.at[k, sem], self.at.pair).wait_recv()
+
+    def step1(self, k):
+        at = self.at
+        mine = at.block(at.p, 0)
+        self.push(k, mine, 0, at.pair)
+        self.push(k, mine, 1, at.follow)
+        self.push(k, mine, 2, at.prev)
+
+    def step2(self, k):
+        at = self.at
+        block = at.block(1 - at.p, 0)
+        self.arrived(k, block, 0, at.core)
+        self.push(k, block, 3, at.follow)
+        self.push(k, block, 4, at.prev)
+        self.share(k, 0)
+
+    def step3(self, k):
+        at = self.at
+        left, right = at.block(at.p, -1), at.block(at.p, 1)
+        self.arrived(k, left, 1, at.core)
+        self.hand(k, self.ref(k, at.core, left).at[FRONT], 5, at.follow)
+        self.arrived(k, right, 2, at.core)
+        self.hand(k, self.ref(k, at.core, right).at[BACK], 6, at.prev)
+
+    def step4(self, k):
+        at = self.at
+        self.arrived(k, at.block(1 - at.p, -1), 3, at.core)
+        self.share(k, -1)
+        self.arrived(k, at.block(1 - at.p, 1), 4, at.core)
+        self.share(k, 1)
+
+    def far1(self, k):
+        at = self.at
+        block = at.block(at.p, 2)
+        self.landed(k, self.ref(k, at.core, block).at[FRONT], 5)
+        self.landed(k, self.ref(k, at.core, block).at[BACK], 6)
+        self.push(k, block, 11, at.pair)
+
+    def far2(self, k):
+        at = self.at
+        self.arrived(k, at.block(1 - at.p, 2), 11, at.core)
+        self.share(k, 2)
 
 
 def layer_kernel(
@@ -259,6 +371,7 @@
     far_a,
     near_a,
     last_a,
+    first_b,
     far_b,
     near_b,
     last_b,
@@ -327,14 +440,19 @@
     barrier = pltpu.get_barrier_semaphore()
     for device in (along_x.prev, along_x.follow, along_x.pair, along_z.prev, along_z.follow, along_z.pair, sib):
         pl.semaphore_signal(barrier, inc=1, device_id=device, device_id_type=MESH)
+    visible[...] = visible_nodes(parents[...], tree_size[0])
     pl.semaphore_wait(barrier, 7)
 
+    side = width // 1
+    halves = [pl.ds(at, side) for at in range(0, width, side)]
+    quarters = [pl.ds(at, min(TILE, sums.shape[-1] - at)) for at in range(0, sums.shape[-1], TILE)]
+    assert len(quarters) == PIECES
     gather_a = Gather(along_z, lambda k, c, b: attn_all.at[k, b, c], ga_send, ga_recv)
     gather_b = Gather(along_x, lambda k, c, b: normed_all.at[k, c, b], gb_send, gb_recv)
-    gather_c = Gather(along_z, lambda k, c, b: hidden_all.at[k, c, b], gc_send, gc_recv)
-    scatter_a = Scatter(along_x, lambda k: proj.at[k], far_a, near_a, last_a, sa_send, sa_recv)
-    scatter_b = Scatter(along_z, lambda k: sums.at[k % 2], far_b, near_b, last_b, sb_send, sb_recv)
-    scatter_c = Scatter(along_x, lambda k: proj.at[k], far_c, near_c, last_c, sc_send, sc_recv)
+    gather_c = PairGather(along_z, lambda k, c, b: hidden_all.at[k, c, b], gc_send, gc_recv)
+    scatter_a = Scatter(along_x, lambda k: proj.at[k], (far_a, near_a, last_a), sa_send, sa_recv, halves)
+    scatter_b = PairScatter(along_z, lambda k: sums.at[k % 2], (first_b, far_b, near_b, last_b), sb_send, sb_recv, quarters)
+    scatter_c = Scatter(along_x, lambda k: proj.at[k], (far_c, near_c, last_c), sc_send, sc_recv, halves)
 
     swaps = [
         remote(
@@ -346,8 +464,8 @@
         )
         for n, w in enumerate((w_gate, w_up))
     ]
-
-    visible[...] = visible_nodes(parents[...], tree_size[0])
+    for copy in swaps:
+        copy.start()
 
     def start(k):
         nodes = slice(k * NODES, (k + 1) * NODES)
@@ -368,14 +486,12 @@
             ),
             wo,
             proj.at[k],
+            side,
+            lambda j: scatter_a.step1(k, j),
         )
-        scatter_a.step1(k)
-        if k == 0:
-            for copy in swaps:
-                copy.start()
 
     def norm(k):
-        projected = scatter_a.step4(k)
+        projected = scatter_a.total(k)
         rows = jnp.concatenate([resid[r * MAXTREE + k * NODES : r * MAXTREE + (k + 1) * NODES, :] for r in (0, 1)], axis=0)
         value = (rows.astype(F32) + projected).astype(BF)
         hid[k] = value
@@ -396,6 +512,8 @@
         if k >= 2:
             scatter_b.close(k - 2)
         part = sums.at[k % 2]
+        squares = normed_all[k, 0, :, :, width:].astype(F32) + normed_all[k, 1, :, :, width:].astype(F32)
+        part[:, :, 2 * half :] = squares.astype(BF)
 
         multiply(
             lambda: jnp.concatenate(
@@ -403,13 +521,12 @@
             ),
             wgu,
             part,
+            TILE,
+            lambda j: scatter_b.step1(k, j),
         )
-        squares = normed_all[k, 0, :, :, width:].astype(F32) + normed_all[k, 1, :, :, width:].astype(F32)
-        part[:, :, 2 * half :] = squares.astype(BF)
-        scatter_b.step1(k)
 
     def activate(k):
-        total = scatter_b.step4(k)
+        total = scatter_b.total(k)
         scale = lax.rsqrt(total[:, 2 * half : 2 * half + 1] / D + EPSILON)
         gate = total[:, 0:half] * scale
         up = total[:, half : 2 * half] * scale
@@ -423,12 +540,15 @@
         scatter_a.close(k)
 
         multiply(
-            lambda: jnp.concatenate([hidden_all[k, c].reshape(ROWS, half) for c in (0, 1)], axis=1), wd, proj.at[k]
+            lambda: jnp.concatenate([hidden_all[k, c].reshape(ROWS, half) for c in (0, 1)], axis=1),
+            wd,
+            proj.at[k],
+            side,
+            lambda j: scatter_c.step1(k, j),
         )
-        scatter_c.step1(k)
 
     def finish(k):
-        total = (hid[k].astype(F32) + scatter_c.step4(k)).astype(BF)
+        total = (hid[k].astype(F32) + scatter_c.total(k)).astype(BF)
         for r in (0, 1):
             out[r * MAXTREE + k * NODES : r * MAXTREE + (k + 1) * NODES, :] = total[r * NODES : (r + 1) * NODES, :]
 
@@ -447,10 +567,13 @@
         gate_up,
         scatter_b.step2,
         scatter_b.step3,
+        scatter_b.step4,
         activate,
         gather_c.step2,
         gather_c.step3,
         gather_c.step4,
+        gather_c.far1,
+        gather_c.far2,
         down,
         scatter_c.step2,
         scatter_c.step3,
@@ -465,10 +588,11 @@
 
 
 TURNS = (
-    0, 1, 0, 3, 0, 1, 2, 0, 1, 0, 2, 1, 0, 1, 2, 3, 0, 1, 2, 3, 0, 2,
-    1, 3, 0, 2, 0, 1, 3, 0, 2, 1, 0, 1, 2, 3, 1, 2, 0, 3, 1, 2, 0, 3,
-    2, 1, 0, 2, 1, 3, 3, 0, 3, 1, 2, 0, 3, 2, 0, 3, 0, 2, 1, 3, 2, 1,
-    0, 2, 3, 1, 0, 2, 3, 1, 3, 2, 1, 3, 2, 3, 1, 3, 2, 0, 3, 2, 1, 3,
+    0, 1, 0, 2, 1, 0, 2, 0, 1, 0, 1, 2, 0, 2, 1, 0, 3, 1, 0, 2, 1, 0, 3, 2,
+    0, 1, 3, 0, 2, 3, 1, 0, 1, 2, 0, 3, 1, 0, 0, 3, 1, 2, 0, 2, 3, 1, 0, 1,
+    2, 1, 3, 2, 3, 1, 3, 2, 0, 2, 0, 1, 1, 3, 3, 0, 1, 2, 1, 3, 3, 2, 3, 2,
+    0, 2, 3, 1, 0, 2, 3, 2, 1, 3, 2, 0, 3, 3, 2, 3, 0, 1, 2, 3, 1, 2, 3, 3,
+    1, 2, 0, 3,
 )
 
 
@@ -482,9 +606,11 @@
     hbm = pl.BlockSpec(memory_space=pl.ANY)
     sem = pltpu.SemaphoreType.DMA
 
-    def scatter_buffers(lanes):
+    def scatter_buffers(lanes, pair):
+        first = [pltpu.VMEM((CHUNKS, BLOCK, lanes), BF)] if pair else []
         return [
-            pltpu.VMEM((CHUNKS, 2, BLOCK, lanes), BF),
+            *first,
+            pltpu.VMEM((CHUNKS, 2, BLOCK // 2 if pair else BLOCK, lanes), BF),
             pltpu.VMEM((CHUNKS, 2, 2, BLOCK, lanes), BF),
             pltpu.VMEM((CHUNKS, BLOCK, lanes), BF),
         ]
@@ -500,14 +626,14 @@
         pltpu.VMEM((2, 8, BLOCK, sums), BF),
         pltpu.VMEM((CHUNKS, 2, 8, BLOCK, half), BF),
         pltpu.VMEM((MAXTREE, MAXTREE), F32),
-        *scatter_buffers(width),
-        *scatter_buffers(sums),
-        *scatter_buffers(width),
+        *scatter_buffers(width, False),
+        *scatter_buffers(sums, True),
+        *scatter_buffers(width, False),
         sem((4,)),
         sem((2,)),
         sem((2,)),
-        *[sem((CHUNKS, 11))] * 6,
-        *[sem((CHUNKS, 7))] * 6,
+        *[sem((CHUNKS, 12))] * 6,
+        *[sem((CHUNKS * PIECES, 10))] * 6,
     ]
     return pl.pallas_call(
         layer_kernel,

time: 168 us -> 163 us (0.970)
  Pallas kernels: 163 us -> 159 us
    pallas_call x1, Pallas kernels: 163 us -> 159 us  [layer(): pl.pallas_call(layer_kernel, out_shape=jax.ShapeDtypeStruct(resid.shape,...]
where the time goes in v5:
time: 163 us; the launch traced here: 162 us
  Pallas kernels  159 us (98%)
  local copies, waits for them, and re-layouts  1.67 us (1%)
    pallas_call x1, Pallas kernels, layer(): pl.pallas_call(layer_kernel, out_shape=jax.ShapeDtypeStruct(resid.shape,...  159 us

profile of v5, /device:TPU:0, one launch (start us, length us, event | category | flops | bytes accessed | tf_op | source)
XLA Modules:
  0.0 162.5 jit_solution(9568987847117802109)
XLA Ops:
  1.3 159.5 %shard_map.127 = bf16[128,1024]{1,0:T(8,128)(2,1)} custom-call(s32[1,8]{1,0:T(1,128)} %page_table.1, s32[1]{0:T(128)S(6)} %copy.15.cache_len, s32[1]{0:T(128)S(6)} %copy.16.tree_size, s32[1,64]{1,0:T(1,128)} %parents.1, bf16[64,2048]{1,0:T(8,128)(2,1)} %queries.1, bf16[64,256]{1,0:T(8,128)(2,1)} %tree_kv.1, bf16[1,8,128,256]{3,2,1,0:T(8,128)(2,1)} %cache.1, ...), custom_call_target="tpu_custom_call" | custom-call | flops 25232932864 | bytes 27262976 | tf_op jit(solution)/shard_map/pallas_call | solution.py:638
  160.8 1.7 %copy.17 = bf16[128,1024]{1,0:T(8,128)(2,1)} copy(bf16[128,1024]{1,0:T(8,128)(2,1)} %shard_map.127) | data formatting | bytes 524288

commit v6 on v5

--- a/solution.py
+++ b/solution.py
@@ -21,8 +21,11 @@
 BLOCK = 2 * NODES
 ROWS = 8 * BLOCK
 LANES = 128
+GROUP = 4
 FRONT, BACK = pl.ds(0, BLOCK // 2), pl.ds(BLOCK // 2, BLOCK // 2)
 TILE = 1024
+INNER = 512
+STRIP = 384
 PIECES = 4
 
 
@@ -40,14 +43,9 @@
     return jnp.where(column < tree_len, turned, 0.0)
 
 
-def attend(query, visible, live, cached, tree_kv, cache, page_table):
-    heads = query.shape[1] // HD
-    keys = jnp.concatenate([query[:, h * HD : (h + 1) * HD] for h in range(heads)], axis=0)
+def attend(queries, nodes, visible, live, cached, tree_kv, cache, page_table, out):
     contract = (((1,), (1,)), ((), ()))
-    context = cache[0].reshape(MAXPAGES * PAGE, 2 * HD)
     scale = HD ** (-0.5)
-    ctx_scores = lax.dot_general(keys, context[:, 0:HD], contract, preferred_element_type=F32) * scale
-    tree_scores = lax.dot_general(keys, tree_kv[:, 0:HD], contract, preferred_element_type=F32) * scale
     offset = lax.broadcasted_iota(jnp.int32, (1, PAGE), 1)
     bounds = []
     for page in range(MAXPAGES):
@@ -56,21 +54,32 @@
             place = jnp.where(page_table[0, p] == page, p, place)
         bounds.append(offset < cached - place * PAGE)
     allowed = jnp.concatenate([jnp.where(bound, 1.0, 0.0) for bound in bounds], axis=1)
-    ctx_scores = jnp.where(allowed > 0.5, ctx_scores, -1e30)
-    seen = jnp.concatenate([visible] * heads, axis=0)
-    tree_scores = jnp.where(seen > 0.5, tree_scores, -1e30)
-    row_max = jnp.maximum(
-        jnp.max(ctx_scores, axis=-1, keepdims=True), jnp.max(tree_scores, axis=-1, keepdims=True)
-    )
-    ctx_exp = jnp.exp(ctx_scores - row_max)
-    tree_exp = jnp.exp(tree_scores - row_max)
-    total = jnp.sum(ctx_exp, axis=-1, keepdims=True) + jnp.sum(tree_exp, axis=-1, keepdims=True)
-    share = 1.0 / total
-    mixed = jnp.dot((ctx_exp * share).astype(BF), context[:, HD:], preferred_element_type=F32)
-    mixed += jnp.dot((tree_exp * share).astype(BF), tree_kv[:, HD:], preferred_element_type=F32)
-    count = query.shape[0]
-    parts = [jnp.where(live, mixed[h * count : (h + 1) * count, :], 0.0).astype(BF) for h in range(heads)]
-    return jnp.concatenate(parts, axis=1)
+    seen = jnp.concatenate([visible] * GROUP, axis=0)
+
+    def group(g, carry):
+        columns = pl.ds(pl.multiple_of(g * GROUP * HD, LANES), GROUP * HD)
+        query = queries[nodes, columns]
+        rows = jnp.concatenate([query[:, h * HD : (h + 1) * HD] for h in range(GROUP)], axis=0)
+        keys = cache[0, :, :, 0:HD].reshape(MAXPAGES * PAGE, HD)
+        ctx_scores = lax.dot_general(rows, keys, contract, preferred_element_type=F32) * scale
+        tree_scores = lax.dot_general(rows, tree_kv[:, 0:HD], contract, preferred_element_type=F32) * scale
+        ctx_scores = jnp.where(allowed > 0.5, ctx_scores, -1e30)
+        tree_scores = jnp.where(seen > 0.5, tree_scores, -1e30)
+        row_max = jnp.maximum(
+            jnp.max(ctx_scores, axis=-1, keepdims=True), jnp.max(tree_scores, axis=-1, keepdims=True)
+        )
+        ctx_exp = jnp.exp(ctx_scores - row_max)
+        tree_exp = jnp.exp(tree_scores - row_max)
+        total = jnp.sum(ctx_exp, axis=-1, keepdims=True) + jnp.sum(tree_exp, axis=-1, keepdims=True)
+        share = 1.0 / total
+        values = cache[0, :, :, HD:].reshape(MAXPAGES * PAGE, HD)
+        mixed = jnp.dot((ctx_exp * share).astype(BF), values, preferred_element_type=F32)
+        mixed += jnp.dot((tree_exp * share).astype(BF), tree_kv[:, HD:], preferred_element_type=F32)
+        parts = [jnp.where(live, mixed[h * NODES : (h + 1) * NODES, :], 0.0).astype(BF) for h in range(GROUP)]
+        out[:, columns] = jnp.concatenate(parts, axis=1)
+        return carry
+
+    lax.fori_loop(0, queries.shape[1] // (GROUP * HD), group, 0)
 
 
 def remote(src, dst, send_sem, recv_sem, device):
@@ -86,11 +95,41 @@
 
 def multiply(rows, weights, result, tile, done):
     width = weights.shape[1]
-    for j, at in enumerate(range(0, width, tile)):
-        size = min(tile, width - at)
-        product = jnp.dot(rows(), weights[:, at : at + size], preferred_element_type=F32)
-        result[:, :, at : at + size] = product.astype(BF).reshape(8, BLOCK, size)
+
+    def columns(at, size):
+        product = jnp.dot(rows(), weights[:, pl.ds(at, size)], preferred_element_type=F32)
+        result[:, :, pl.ds(at, size)] = product.astype(BF).reshape(8, BLOCK, size)
+
+    for j, start in enumerate(range(0, width, tile)):
+        size = min(tile, width - start)
+        whole = size // INNER
+
+        def step(n, carry, start=start):
+            columns(pl.multiple_of(start + n * INNER, LANES), INNER)
+            return carry
+
+        if whole:
+            lax.fori_loop(0, whole, step, 0)
+        if size % INNER:
+            columns(start + whole * INNER, size % INNER)
         done(j)
+
+
+def strips(width, size, work):
+    def step(n, carry):
+        work(pl.ds(pl.multiple_of(n * size, LANES), size))
+        return carry
+
+    lax.fori_loop(0, width // size, step, 0)
+    if width % size:
+        work(pl.ds(width - width % size, width % size))
+
+
+def accumulate(target, source):
+    def work(columns):
+        target[:, columns] = (target[:, columns].astype(F32) + source[:, columns].astype(F32)).astype(BF)
+
+    strips(target.shape[1], STRIP, work)
 
 
 class Place:
@@ -146,15 +185,26 @@
         for way, (p, shift, device, sem) in enumerate(((0, 1, at.follow, 2), (1, -1, at.prev, 5))):
             self.arrived(k, self.far.at[k, way], way, True)
             mine = at.block(p, shift)
-            part[mine] = (part[mine].astype(F32) + self.far[k, way].astype(F32)).astype(BF)
+            accumulate(part.at[mine], self.far.at[k, way])
             self.hand(k, part.at[mine], self.near.at[k, way, p], sem, device)
 
-    def ring_sum(self, k, p):
+    def ring_sum(self, k, p, columns):
         return (
-            self.part(k)[self.at.block(p, 0)].astype(F32)
-            + self.near[k, 0, p].astype(F32)
-            + self.near[k, 1, p].astype(F32)
+            self.part(k)[self.at.block(p, 0), :, columns].astype(F32)
+            + self.near[k, 0, p, :, columns].astype(F32)
+            + self.near[k, 1, p, :, columns].astype(F32)
         )
+
+    def pair_sum(self, k, p):
+        ours = self.part(k).at[self.at.block(p, 0)]
+
+        def work(columns):
+            ours[:, columns] = self.ring_sum(k, p, columns).astype(BF)
+
+        strips(ours.shape[1], STRIP, work)
+
+    def total(self, k, columns):
+        return self.ring_sum(k, self.at.p, columns) + self.last[k, :, columns].astype(F32)
 
     def step3(self, k):
         at, part = self.at, self.part(k)
@@ -164,12 +214,11 @@
         self.arrived(k, self.near.at[k, 1, 1], 5)
         other = 1 - at.p
         theirs = at.block(other, 0)
-        part[theirs] = self.ring_sum(k, other).astype(BF)
+        self.pair_sum(k, other)
         self.hand(k, part.at[theirs], self.last.at[k], 6, at.pair)
 
-    def total(self, k):
+    def settle(self, k):
         self.arrived(k, self.last.at[k], 6)
-        return self.ring_sum(k, self.at.p) + self.last[k].astype(F32)
 
     def close(self, k):
         for copy in self.open.pop(k, []):
@@ -196,7 +245,7 @@
         at, part = self.at, self.part(k)
         self.arrived(k, self.first.at[k], 0, True)
         mine = at.block(at.p, 2)
-        part[mine] = (part[mine].astype(F32) + self.first[k].astype(F32)).astype(BF)
+        accumulate(part.at[mine], self.first.at[k])
         self.hand(k, part.at[mine, FRONT], self.far.at[k, 0], 1, at.follow)
         self.hand(k, part.at[mine, BACK], self.far.at[k, 1], 2, at.prev)
 
@@ -206,7 +255,7 @@
         self.arrived(k, self.near.at[k, 0, other], 3, True)
         self.arrived(k, self.near.at[k, 1, other], 4, True)
         theirs = at.block(other, 0)
-        part[theirs] = self.ring_sum(k, other).astype(BF)
+        self.pair_sum(k, other)
         self.hand(k, part.at[theirs], self.last.at[k], 9, at.pair)
 
     def step4(self, k):
@@ -214,16 +263,15 @@
         for way, (shift, rows, sem, device) in enumerate(((1, FRONT, 5, at.follow), (-1, BACK, 7, at.prev))):
             self.arrived(k, self.far.at[k, way], 1 + way)
             mine = at.block(at.p, shift)
-            part[mine, rows] = (part[mine, rows].astype(F32) + self.far[k, way].astype(F32)).astype(BF)
+            accumulate(part.at[mine, rows], self.far.at[k, way])
             self.hand(k, part.at[mine, rows], self.near.at[k, way, at.p, rows], sem, device)
 
-    def total(self, k):
+    def settle(self, k):
         p = self.at.p
         for way, (added, alone) in enumerate(((FRONT, BACK), (BACK, FRONT))):
             self.arrived(k, self.near.at[k, way, p, added], 5 + 2 * way)
             self.arrived(k, self.near.at[k, way, p, alone], 6 + 2 * way, True)
         self.arrived(k, self.last.at[k], 9)
-        return self.ring_sum(k, p) + self.last[k].astype(F32)
 
 
 class Gather:
@@ -470,8 +518,16 @@
     def start(k):
         nodes = slice(k * NODES, (k + 1) * NODES)
         node = lax.broadcasted_iota(jnp.int32, (NODES, 1), 0) + k * NODES
-        attn_all[k, along_z.block(yl, 0), core] = attend(
-            queries[nodes, :], visible[nodes, :], node < tree_size[0], cache_len[0], tree_kv[...], cache, page_table
+        attend(
+            queries,
+            nodes,
+            visible[nodes, :],
+            node < tree_size[0],
+            cache_len[0],
+            tree_kv,
+            cache,
+            page_table,
+            attn_all.at[k, along_z.block(yl, 0), core],
         )
         gather_a.step1(k)
 
@@ -491,14 +547,20 @@
         )
 
     def norm(k):
-        projected = scatter_a.total(k)
-        rows = jnp.concatenate([resid[r * MAXTREE + k * NODES : r * MAXTREE + (k + 1) * NODES, :] for r in (0, 1)], axis=0)
-        value = (rows.astype(F32) + projected).astype(BF)
-        hid[k] = value
-        wide = value.astype(F32)
+        scatter_a.settle(k)
         mine = along_x.block(yh, 0)
-        normed_all[k, core, mine, :, 0:width] = (wide * gain[...].astype(F32).reshape(1, width)).astype(BF)
-        squares = jnp.sum(wide * wide, axis=1, keepdims=True)
+        squares = jnp.zeros((BLOCK, 1), F32)
+        for at in range(0, width, 512):
+            columns = pl.ds(at, 512)
+            rows = jnp.concatenate(
+                [resid[r * MAXTREE + k * NODES : r * MAXTREE + (k + 1) * NODES, columns] for r in (0, 1)], axis=0
+            )
+            value = (rows.astype(F32) + scatter_a.total(k, columns)).astype(BF)
+            hid[k, :, columns] = value
+            wide = value.astype(F32)
+            scaled = wide * gain[at : at + 512].astype(F32).reshape(1, 512)
+            normed_all[k, core, mine, :, columns] = scaled.astype(BF)
+            squares += jnp.sum(wide * wide, axis=1, keepdims=True)
         normed_all[k, core, mine, :, width:] = jnp.broadcast_to(squares, (BLOCK, LANES)).astype(BF)
         gather_b.step1(k)
 
@@ -526,11 +588,17 @@
         )
 
     def activate(k):
-        total = scatter_b.total(k)
-        scale = lax.rsqrt(total[:, 2 * half : 2 * half + 1] / D + EPSILON)
-        gate = total[:, 0:half] * scale
-        up = total[:, half : 2 * half] * scale
-        hidden_all[k, core, along_z.block(yl, 0)] = (gate / (1.0 + jnp.exp(-gate)) * up).astype(BF)
+        scatter_b.settle(k)
+        squares = scatter_b.total(k, pl.ds(2 * half, LANES))[:, 0:1]
+        scale = lax.rsqrt(squares / D + EPSILON)
+        mine = along_z.block(yl, 0)
+
+        def work(columns):
+            gate = scatter_b.total(k, columns) * scale
+            up = scatter_b.total(k, pl.ds(half + columns.start, columns.size)) * scale
+            hidden_all[k, core, mine, :, columns] = (gate / (1.0 + jnp.exp(-gate)) * up).astype(BF)
+
+        strips(half, 256, work)
         gather_c.step1(k)
 
     def down(k):
@@ -548,9 +616,13 @@
         )
 
     def finish(k):
-        total = (hid[k].astype(F32) + scatter_c.total(k)).astype(BF)
-        for r in (0, 1):
-            out[r * MAXTREE + k * NODES : r * MAXTREE + (k + 1) * NODES, :] = total[r * NODES : (r + 1) * NODES, :]
+        scatter_c.settle(k)
+        for at in range(0, width, 512):
+            columns = pl.ds(at, 512)
+            total = (hid[k, :, columns].astype(F32) + scatter_c.total(k, columns)).astype(BF)
+            for r in (0, 1):
+                rows = slice(r * MAXTREE + k * NODES, r * MAXTREE + (k + 1) * NODES)
+                out[rows, columns] = total[r * NODES : (r + 1) * NODES, :]
 
     stages = [
         start,

time: 163 us -> 165 us (1.012)
  Pallas kernels: 159 us -> 162 us
    pallas_call x1, Pallas kernels: 159 us -> 162 us  [layer(): pl.pallas_call(layer_kernel, out_shape=jax.ShapeDtypeStruct(resid.shape,...]
where the time goes in v6:
time: 165 us
  Pallas kernels  162 us (98%)
  local copies, waits for them, and re-layouts  1.67 us (1%)
    pallas_call x1, Pallas kernels, layer(): pl.pallas_call(layer_kernel, out_shape=jax.ShapeDtypeStruct(resid.shape,...  162 us

profile of v6, /device:TPU:0, one launch (start us, length us, event | category | flops | bytes accessed | tf_op | source)
XLA Modules:
  0.0 164.9 jit_solution(7395840538870257836)
XLA Ops:
  1.3 162.0 %shard_map.127 = bf16[128,1024]{1,0:T(8,128)(2,1)} custom-call(s32[1,8]{1,0:T(1,128)} %page_table.1, s32[1]{0:T(128)S(6)} %copy.15.cache_len, s32[1]{0:T(128)S(6)} %copy.16.tree_size, s32[1,64]{1,0:T(1,128)} %parents.1, bf16[64,2048]{1,0:T(8,128)(2,1)} %queries.1, bf16[64,256]{1,0:T(8,128)(2,1)} %tree_kv.1, bf16[1,8,128,256]{3,2,1,0:T(8,128)(2,1)} %cache.1, ...), custom_call_target="tpu_custom_call" | custom-call | flops 25232932864 | bytes 27262976 | tf_op jit(solution)/shard_map/pallas_call | solution.py:710
  163.3 1.7 %copy.17 = bf16[128,1024]{1,0:T(8,128)(2,1)} copy(bf16[128,1024]{1,0:T(8,128)(2,1)} %shard_map.127) | data formatting | bytes 524288

commit v7 on v5

--- a/solution.py
+++ b/solution.py
@@ -93,6 +93,11 @@
         done(j)
 
 
+def other_core(device):
+    gx, gy = device
+    return gx, gy + 1 - 2 * lax.rem(gy, 2)
+
+
 class Place:
     def __init__(self, r, p, prev, follow, pair, sib, core, index):
         self.r, self.p = r, p
@@ -289,6 +294,30 @@
     def close(self, k):
         for copy in self.open.pop(k, []):
             copy.wait_send()
+
+
+class FarGather(Gather):
+    def step3(self, k):
+        at = self.at
+        left, right = at.block(0, -1), at.block(1, 1)
+        self.arrived(k, left, 1, at.core)
+        self.push(k, left, 5, at.follow)
+        self.push(k, left, 12, other_core(at.follow))
+        self.arrived(k, right, 4, at.core)
+        self.push(k, right, 6, at.prev)
+        self.push(k, right, 13, other_core(at.prev))
+        self.arrived(k, at.block(1, -1), 2, at.core)
+        self.share(k, -1)
+        self.arrived(k, at.block(0, 1), 3, at.core)
+        self.share(k, 1)
+
+    def step5(self, k):
+        at = self.at
+        for shift in (0, 1, -1):
+            self.arrived(k, self.both(shift), 7 + shift % 4, 1 - at.core)
+        for core, sems in ((at.core, (5, 6)), (1 - at.core, (12, 13))):
+            self.arrived(k, at.block(0, 2), sems[0], core)
+            self.arrived(k, at.block(1, 2), sems[1], core)
 
 
 class PairGather(Gather):
@@ -368,6 +397,7 @@
     sums,
     hidden_all,
     visible,
+    first_a,
     far_a,
     near_a,
     last_a,
@@ -375,6 +405,7 @@
     far_b,
     near_b,
     last_b,
+    first_c,
     far_c,
     near_c,
     last_c,
@@ -438,21 +469,24 @@
     load(w_down, wd)
 
     barrier = pltpu.get_barrier_semaphore()
-    for device in (along_x.prev, along_x.follow, along_x.pair, along_z.prev, along_z.follow, along_z.pair, sib):
+    near = [sib, other_core(along_z.prev), other_core(along_z.follow)]
+    for place in (along_x, along_z):
+        near += [place.prev, place.follow, place.pair]
+    for device in near:
         pl.semaphore_signal(barrier, inc=1, device_id=device, device_id_type=MESH)
     visible[...] = visible_nodes(parents[...], tree_size[0])
-    pl.semaphore_wait(barrier, 7)
+    pl.semaphore_wait(barrier, len(near))
 
     side = width // 1
     halves = [pl.ds(at, side) for at in range(0, width, side)]
     quarters = [pl.ds(at, min(TILE, sums.shape[-1] - at)) for at in range(0, sums.shape[-1], TILE)]
     assert len(quarters) == PIECES
-    gather_a = Gather(along_z, lambda k, c, b: attn_all.at[k, b, c], ga_send, ga_recv)
+    gather_a = FarGather(along_z, lambda k, c, b: attn_all.at[k, b, c], ga_send, ga_recv)
     gather_b = Gather(along_x, lambda k, c, b: normed_all.at[k, c, b], gb_send, gb_recv)
     gather_c = PairGather(along_z, lambda k, c, b: hidden_all.at[k, c, b], gc_send, gc_recv)
-    scatter_a = Scatter(along_x, lambda k: proj.at[k], (far_a, near_a, last_a), sa_send, sa_recv, halves)
+    scatter_a = PairScatter(along_x, lambda k: proj.at[k], (first_a, far_a, near_a, last_a), sa_send, sa_recv, halves)
     scatter_b = PairScatter(along_z, lambda k: sums.at[k % 2], (first_b, far_b, near_b, last_b), sb_send, sb_recv, quarters)
-    scatter_c = Scatter(along_x, lambda k: proj.at[k], (far_c, near_c, last_c), sc_send, sc_recv, halves)
+    scatter_c = PairScatter(along_x, lambda k: proj.at[k], (first_c, far_c, near_c, last_c), sc_send, sc_recv, halves)
 
     swaps = [
         remote(
@@ -556,10 +590,10 @@
         start,
         gather_a.step2,
         gather_a.step3,
-        gather_a.step4,
         project,
         scatter_a.step2,
         scatter_a.step3,
+        scatter_a.step4,
         norm,
         gather_b.step2,
         gather_b.step3,
@@ -577,6 +611,7 @@
         down,
         scatter_c.step2,
         scatter_c.step3,
+        scatter_c.step4,
         finish,
     ]
     ahead = [iter(stages) for k in range(CHUNKS)]
@@ -588,11 +623,11 @@
 
 
 TURNS = (
-    0, 1, 0, 2, 1, 0, 2, 0, 1, 0, 1, 2, 0, 2, 1, 0, 3, 1, 0, 2, 1, 0, 3, 2,
-    0, 1, 3, 0, 2, 3, 1, 0, 1, 2, 0, 3, 1, 0, 0, 3, 1, 2, 0, 2, 3, 1, 0, 1,
-    2, 1, 3, 2, 3, 1, 3, 2, 0, 2, 0, 1, 1, 3, 3, 0, 1, 2, 1, 3, 3, 2, 3, 2,
-    0, 2, 3, 1, 0, 2, 3, 2, 1, 3, 2, 0, 3, 3, 2, 3, 0, 1, 2, 3, 1, 2, 3, 3,
-    1, 2, 0, 3,
+    0, 3, 0, 1, 0, 2, 1, 0, 2, 1, 0, 0, 2, 0, 1, 0, 3, 1, 1, 0, 1, 2, 3, 0,
+    1, 2, 0, 2, 1, 0, 2, 3, 1, 2, 0, 0, 3, 1, 3, 2, 0, 1, 2, 3, 0, 2, 3, 1,
+    2, 1, 3, 1, 3, 0, 2, 3, 0, 1, 3, 2, 0, 3, 2, 0, 3, 1, 3, 2, 0, 1, 3, 2,
+    1, 2, 1, 0, 3, 2, 3, 2, 1, 3, 0, 3, 2, 1, 0, 0, 3, 2, 1, 3, 1, 2, 1, 2,
+    3, 2, 3, 3, 1, 2, 0, 3,
 )
 
 
@@ -626,13 +661,13 @@
         pltpu.VMEM((2, 8, BLOCK, sums), BF),
         pltpu.VMEM((CHUNKS, 2, 8, BLOCK, half), BF),
         pltpu.VMEM((MAXTREE, MAXTREE), F32),
-        *scatter_buffers(width, False),
+        *scatter_buffers(width, True),
         *scatter_buffers(sums, True),
-        *scatter_buffers(width, False),
+        *scatter_buffers(width, True),
         sem((4,)),
         sem((2,)),
         sem((2,)),
-        *[sem((CHUNKS, 12))] * 6,
+        *[sem((CHUNKS, 14))] * 6,
         *[sem((CHUNKS * PIECES, 10))] * 6,
     ]
     return pl.pallas_call(

time: 163 us -> 161 us (0.988)
  Pallas kernels: 159 us -> 157 us
    pallas_call x1, Pallas kernels: 159 us -> 157 us  [layer(): pl.pallas_call(layer_kernel, out_shape=jax.ShapeDtypeStruct(resid.shape,...]
where the time goes in v7:
time: 161 us; the launch traced here: 160 us
  Pallas kernels  157 us (98%)
  local copies, waits for them, and re-layouts  1.67 us (1%)
    pallas_call x1, Pallas kernels, layer(): pl.pallas_call(layer_kernel, out_shape=jax.ShapeDtypeStruct(resid.shape,...  157 us

profile of v7, /device:TPU:0, one launch (start us, length us, event | category | flops | bytes accessed | tf_op | source)
XLA Modules:
  0.0 160.4 jit_solution(17713825508347358555)
XLA Ops:
  1.3 157.4 %shard_map.127 = bf16[128,1024]{1,0:T(8,128)(2,1)} custom-call(s32[1,8]{1,0:T(1,128)} %page_table.1, s32[1]{0:T(128)S(6)} %copy.15.cache_len, s32[1]{0:T(128)S(6)} %copy.16.tree_size, s32[1,64]{1,0:T(1,128)} %parents.1, bf16[64,2048]{1,0:T(8,128)(2,1)} %queries.1, bf16[64,256]{1,0:T(8,128)(2,1)} %tree_kv.1, bf16[1,8,128,256]{3,2,1,0:T(8,128)(2,1)} %cache.1, ...), custom_call_target="tpu_custom_call" | custom-call | flops 25232932864 | bytes 27262976 | tf_op jit(solution)/shard_map/pallas_call | solution.py:673
  158.7 1.7 %copy.17 = bf16[128,1024]{1,0:T(8,128)(2,1)} copy(bf16[128,1024]{1,0:T(8,128)(2,1)} %shard_map.127) | data formatting | bytes 524288

commit v8 on v7

--- a/solution.py
+++ b/solution.py
@@ -1,3 +1,5 @@
+import math
+
 import jax
 import jax.numpy as jnp
 from jax import lax
@@ -45,9 +47,9 @@
     keys = jnp.concatenate([query[:, h * HD : (h + 1) * HD] for h in range(heads)], axis=0)
     contract = (((1,), (1,)), ((), ()))
     context = cache[0].reshape(MAXPAGES * PAGE, 2 * HD)
-    scale = HD ** (-0.5)
-    ctx_scores = lax.dot_general(keys, context[:, 0:HD], contract, preferred_element_type=F32) * scale
-    tree_scores = lax.dot_general(keys, tree_kv[:, 0:HD], contract, preferred_element_type=F32) * scale
+    scale = HD ** (-0.5) * math.log2(math.e)
+    ctx_scores = lax.dot_general(keys, context[:, 0:HD], contract, preferred_element_type=F32)
+    tree_scores = lax.dot_general(keys, tree_kv[:, 0:HD], contract, preferred_element_type=F32)
     offset = lax.broadcasted_iota(jnp.int32, (1, PAGE), 1)
     bounds = []
     for page in range(MAXPAGES):
@@ -62,12 +64,12 @@
     row_max = jnp.maximum(
         jnp.max(ctx_scores, axis=-1, keepdims=True), jnp.max(tree_scores, axis=-1, keepdims=True)
     )
-    ctx_exp = jnp.exp(ctx_scores - row_max)
-    tree_exp = jnp.exp(tree_scores - row_max)
+    ctx_exp = jnp.exp2((ctx_scores - row_max) * scale)
+    tree_exp = jnp.exp2((tree_scores - row_max) * scale)
     total = jnp.sum(ctx_exp, axis=-1, keepdims=True) + jnp.sum(tree_exp, axis=-1, keepdims=True)
-    share = 1.0 / total
-    mixed = jnp.dot((ctx_exp * share).astype(BF), context[:, HD:], preferred_element_type=F32)
-    mixed += jnp.dot((tree_exp * share).astype(BF), tree_kv[:, HD:], preferred_element_type=F32)
+    mixed = jnp.dot(ctx_exp.astype(BF), context[:, HD:], preferred_element_type=F32)
+    mixed += jnp.dot(tree_exp.astype(BF), tree_kv[:, HD:], preferred_element_type=F32)
+    mixed *= 1.0 / total
     count = query.shape[0]
     parts = [jnp.where(live, mixed[h * count : (h + 1) * count, :], 0.0).astype(BF) for h in range(heads)]
     return jnp.concatenate(parts, axis=1)
@@ -475,6 +477,15 @@
     for device in near:
         pl.semaphore_signal(barrier, inc=1, device_id=device, device_id_type=MESH)
     visible[...] = visible_nodes(parents[...], tree_size[0])
+
+    def attention(k):
+        nodes = slice(k * NODES, (k + 1) * NODES)
+        node = lax.broadcasted_iota(jnp.int32, (NODES, 1), 0) + k * NODES
+        attn_all[k, along_z.block(yl, 0), core] = attend(
+            queries[nodes, :], visible[nodes, :], node < tree_size[0], cache_len[0], tree_kv[...], cache, page_table
+        )
+
+    attention(0)
     pl.semaphore_wait(barrier, len(near))
 
     side = width // 1
@@ -502,11 +513,8 @@
         copy.start()
 
     def start(k):
-        nodes = slice(k * NODES, (k + 1) * NODES)
-        node = lax.broadcasted_iota(jnp.int32, (NODES, 1), 0) + k * NODES
-        attn_all[k, along_z.block(yl, 0), core] = attend(
-            queries[nodes, :], visible[nodes, :], node < tree_size[0], cache_len[0], tree_kv[...], cache, page_table
-        )
+        if k > 0:
+            attention(k)
         gather_a.step1(k)
 
     def project(k):
@@ -623,11 +631,11 @@
 
 
 TURNS = (
-    0, 3, 0, 1, 0, 2, 1, 0, 2, 1, 0, 0, 2, 0, 1, 0, 3, 1, 1, 0, 1, 2, 3, 0,
-    1, 2, 0, 2, 1, 0, 2, 3, 1, 2, 0, 0, 3, 1, 3, 2, 0, 1, 2, 3, 0, 2, 3, 1,
-    2, 1, 3, 1, 3, 0, 2, 3, 0, 1, 3, 2, 0, 3, 2, 0, 3, 1, 3, 2, 0, 1, 3, 2,
-    1, 2, 1, 0, 3, 2, 3, 2, 1, 3, 0, 3, 2, 1, 0, 0, 3, 2, 1, 3, 1, 2, 1, 2,
-    3, 2, 3, 3, 1, 2, 0, 3,
+    0, 1, 0, 3, 1, 0, 2, 1, 3, 2, 0, 1, 0, 0, 2, 3, 1, 1, 0, 1, 0, 1, 2, 0,
+    3, 0, 1, 2, 2, 0, 3, 3, 1, 2, 0, 3, 1, 2, 0, 3, 1, 0, 0, 2, 3, 1, 2, 0,
+    1, 2, 3, 1, 2, 0, 2, 0, 1, 2, 3, 2, 3, 0, 0, 2, 0, 3, 3, 1, 1, 0, 3, 2,
+    1, 2, 1, 3, 1, 0, 2, 2, 3, 0, 3, 1, 2, 3, 3, 2, 1, 3, 1, 0, 3, 2, 2, 3,
+    3, 1, 2, 3, 0, 1, 2, 3,
 )
 
 

time: 161 us -> 161 us (level)
  no operation moved by 1% of the time
where the time goes in v8:
time: 161 us; the launch traced here: 160 us
  Pallas kernels  157 us (98%)
  local copies, waits for them, and re-layouts  1.67 us (1%)
    pallas_call x1, Pallas kernels, layer(): pl.pallas_call(layer_kernel, out_shape=jax.ShapeDtypeStruct(resid.shape,...  157 us

profile of v8, /device:TPU:0, one launch (start us, length us, event | category | flops | bytes accessed | tf_op | source)
XLA Modules:
  0.0 159.8 jit_solution(7692917717147913580)
XLA Ops:
  1.3 156.8 %shard_map.127 = bf16[128,1024]{1,0:T(8,128)(2,1)} custom-call(s32[1,8]{1,0:T(1,128)} %page_table.1, s32[1]{0:T(128)S(6)} %copy.15.cache_len, s32[1]{0:T(128)S(6)} %copy.16.tree_size, s32[1,64]{1,0:T(1,128)} %parents.1, bf16[64,2048]{1,0:T(8,128)(2,1)} %queries.1, bf16[64,256]{1,0:T(8,128)(2,1)} %tree_kv.1, bf16[1,8,128,256]{3,2,1,0:T(8,128)(2,1)} %cache.1, ...), custom_call_target="tpu_custom_call" | custom-call | flops 25232932864 | bytes 27262976 | tf_op jit(solution)/shard_map/pallas_call | solution.py:681
  158.2 1.7 %copy.17 = bf16[128,1024]{1,0:T(8,128)(2,1)} copy(bf16[128,1024]{1,0:T(8,128)(2,1)} %shard_map.127) | data formatting | bytes 524288

commit v9 on v8

--- a/solution.py
+++ b/solution.py
@@ -379,15 +379,20 @@
     cache_len,
     tree_size,
     parents,
-    queries,
-    tree_kv,
-    cache,
-    resid,
+    queries_hbm,
+    tree_kv_hbm,
+    cache_hbm,
+    resid_hbm,
     gain,
     w_out,
     w_gate,
     w_up,
     w_down,
+    out_hbm,
+    queries,
+    tree_kv,
+    cache,
+    resid,
     out,
     wo,
     wgu,
@@ -412,6 +417,7 @@
     near_c,
     last_c,
     load_sem,
+    store_sem,
     swap_send,
     swap_recv,
     ga_send,
@@ -456,6 +462,12 @@
         lambda p, r: r * 2 + p,
     )
 
+    barrier = pltpu.get_barrier_semaphore()
+    near = [sib, other_core(along_z.prev), other_core(along_z.follow)]
+    for place in (along_x, along_z):
+        near += [place.prev, place.follow, place.pair]
+    for device in near:
+        pl.semaphore_signal(barrier, inc=1, device_id=device, device_id_type=MESH)
     loads = []
 
     def load(src, dst):
@@ -463,6 +475,10 @@
         copy.start()
         loads.append(copy)
 
+    load(queries_hbm, queries)
+    load(tree_kv_hbm, tree_kv)
+    load(cache_hbm, cache)
+    load(resid_hbm, resid)
     load(w_out, wo)
     mine, theirs = pl.multiple_of(core * half, LANES), pl.multiple_of((1 - core) * half, LANES)
     deep = pl.ds(pl.multiple_of(core * depth, depth), depth)
@@ -470,12 +486,6 @@
     load(w_up.at[:, pl.ds(mine, half)], wgu.at[deep, pl.ds(half, half)])
     load(w_down, wd)
 
-    barrier = pltpu.get_barrier_semaphore()
-    near = [sib, other_core(along_z.prev), other_core(along_z.follow)]
-    for place in (along_x, along_z):
-        near += [place.prev, place.follow, place.pair]
-    for device in near:
-        pl.semaphore_signal(barrier, inc=1, device_id=device, device_id_type=MESH)
     visible[...] = visible_nodes(parents[...], tree_size[0])
 
     def attention(k):
@@ -485,6 +495,8 @@
             queries[nodes, :], visible[nodes, :], node < tree_size[0], cache_len[0], tree_kv[...], cache, page_table
         )
 
+    for copy in loads[0:3]:
+        copy.wait()
     attention(0)
     pl.semaphore_wait(barrier, len(near))
 
@@ -520,7 +532,7 @@
     def project(k):
         gather_a.step5(k)
         if k == 0:
-            loads[0].wait()
+            loads[4].wait()
 
         multiply(
             lambda: jnp.concatenate(
@@ -533,6 +545,8 @@
         )
 
     def norm(k):
+        if k == 0:
+            loads[3].wait()
         projected = scatter_a.total(k)
         rows = jnp.concatenate([resid[r * MAXTREE + k * NODES : r * MAXTREE + (k + 1) * NODES, :] for r in (0, 1)], axis=0)
         value = (rows.astype(F32) + projected).astype(BF)
@@ -547,8 +561,8 @@
     def gate_up(k):
         gather_b.step5(k)
         if k == 0:
-            loads[1].wait()
-            loads[2].wait()
+            loads[5].wait()
+            loads[6].wait()
             for copy in swaps:
                 copy.wait()
         if k >= 2:
@@ -578,7 +592,7 @@
     def down(k):
         gather_c.step5(k)
         if k == 0:
-            loads[3].wait()
+            loads[7].wait()
         scatter_a.close(k)
 
         multiply(
@@ -589,10 +603,16 @@
             lambda j: scatter_c.step1(k, j),
         )
 
+    stores = []
+
     def finish(k):
         total = (hid[k].astype(F32) + scatter_c.total(k)).astype(BF)
         for r in (0, 1):
-            out[r * MAXTREE + k * NODES : r * MAXTREE + (k + 1) * NODES, :] = total[r * NODES : (r + 1) * NODES, :]
+            rows = slice(r * MAXTREE + k * NODES, r * MAXTREE + (k + 1) * NODES)
+            out[rows, :] = total[r * NODES : (r + 1) * NODES, :]
+            copy = pltpu.make_async_copy(out.at[rows], out_hbm.at[rows], store_sem.at[2 * k + r])
+            copy.start()
+            stores.append(copy)
 
     stages = [
         start,
@@ -628,14 +648,16 @@
     for group in (gather_a, gather_b, gather_c, scatter_a, scatter_b, scatter_c):
         for k in range(CHUNKS):
             group.close(k)
+    for copy in stores:
+        copy.wait()
 
 
 TURNS = (
-    0, 1, 0, 3, 1, 0, 2, 1, 3, 2, 0, 1, 0, 0, 2, 3, 1, 1, 0, 1, 0, 1, 2, 0,
-    3, 0, 1, 2, 2, 0, 3, 3, 1, 2, 0, 3, 1, 2, 0, 3, 1, 0, 0, 2, 3, 1, 2, 0,
-    1, 2, 3, 1, 2, 0, 2, 0, 1, 2, 3, 2, 3, 0, 0, 2, 0, 3, 3, 1, 1, 0, 3, 2,
-    1, 2, 1, 3, 1, 0, 2, 2, 3, 0, 3, 1, 2, 3, 3, 2, 1, 3, 1, 0, 3, 2, 2, 3,
-    3, 1, 2, 3, 0, 1, 2, 3,
+    0, 3, 0, 1, 0, 2, 1, 0, 2, 1, 0, 0, 2, 0, 1, 0, 3, 1, 1, 0, 1, 2, 3, 0,
+    1, 2, 0, 2, 1, 0, 2, 3, 1, 2, 0, 0, 3, 1, 3, 2, 0, 1, 2, 3, 0, 2, 3, 1,
+    2, 1, 3, 1, 3, 0, 2, 3, 0, 1, 3, 2, 0, 3, 2, 0, 3, 1, 3, 2, 0, 1, 3, 2,
+    1, 2, 1, 0, 3, 2, 3, 2, 1, 3, 0, 3, 2, 1, 0, 0, 3, 2, 1, 3, 1, 2, 1, 2,
+    3, 2, 3, 3, 1, 2, 0, 3,
 )
 
 
@@ -659,6 +681,7 @@
         ]
 
     scratch = [
+        *[pltpu.VMEM(a.shape, BF) for a in (queries, tree_kv, cache, resid, resid)],
         pltpu.VMEM((heads, width), BF),
         pltpu.VMEM((2 * depth, units), BF),
         pltpu.VMEM((units, width), BF),
@@ -672,7 +695,8 @@
         *scatter_buffers(width, True),
         *scatter_buffers(sums, True),
         *scatter_buffers(width, True),
-        sem((4,)),
+        sem((8,)),
+        sem((2 * CHUNKS,)),
         sem((2,)),
         sem((2,)),
         *[sem((CHUNKS, 14))] * 6,
@@ -681,8 +705,8 @@
     return pl.pallas_call(
         layer_kernel,
         out_shape=jax.ShapeDtypeStruct(resid.shape, BF),
-        in_specs=[smem, smem, smem, vmem, vmem, vmem, vmem, vmem, vmem, hbm, hbm, hbm, hbm],
-        out_specs=vmem,
+        in_specs=[smem, smem, smem, vmem, hbm, hbm, hbm, hbm, vmem, hbm, hbm, hbm, hbm],
+        out_specs=hbm,
         scratch_shapes=scratch,
         compiler_params=pltpu.CompilerParams(
             collective_id=0, has_side_effects=True, vmem_limit_bytes=62 * 1024 * 1024

time: 161 us -> 159 us (0.988)
  Pallas kernels: 157 us -> 155 us
    pallas_call x1, Pallas kernels: 157 us -> 155 us  [layer(): pl.pallas_call(layer_kernel, out_shape=jax.ShapeDtypeStruct(resid.shape,...]
where the time goes in v9:
time: 159 us; the launch traced here: 158 us
  Pallas kernels  155 us (97%)
  local copies, waits for them, and re-layouts  1.67 us (1%)
    pallas_call x1, Pallas kernels, layer(): pl.pallas_call(layer_kernel, out_shape=jax.ShapeDtypeStruct(resid.shape,...  155 us

profile of v9, /device:TPU:0, one launch (start us, length us, event | category | flops | bytes accessed | tf_op | source)
XLA Modules:
  0.0 158.1 jit_solution(6209076548560807428)
XLA Ops:
  1.3 155.2 %shard_map.127 = bf16[128,1024]{1,0:T(8,128)(2,1)} custom-call(s32[1,8]{1,0:T(1,128)} %page_table.1, s32[1]{0:T(128)S(6)} %copy.15.cache_len, s32[1]{0:T(128)S(6)} %copy.16.tree_size, s32[1,64]{1,0:T(1,128)} %parents.1, bf16[64,2048]{1,0:T(8,128)(2,1)} %queries_hbm.1, bf16[64,256]{1,0:T(8,128)(2,1)} %tree_kv_hbm.1, bf16[1,8,128,256]{3,2,1,0:T(8,128)(2,1)} %cache_hbm.1, ...), custom_call_target="tpu_custom_call" | custom-call | flops 25232932864 | bytes 27262976 | tf_op jit(solution)/shard_map/pallas_call | solution.py:705
  156.5 1.7 %copy.17 = bf16[128,1024]{1,0:T(8,128)(2,1)} copy(bf16[128,1024]{1,0:T(8,128)(2,1)} %shard_map.127) | data formatting | bytes 524288

commit v10 on v9

--- a/solution.py
+++ b/solution.py
@@ -500,16 +500,16 @@
     attention(0)
     pl.semaphore_wait(barrier, len(near))
 
-    side = width // 1
-    halves = [pl.ds(at, side) for at in range(0, width, side)]
+    whole = [pl.ds(0, width)]
+    down_cuts = [pl.ds(at, width // 2) for at in range(0, width, width // 2)]
     quarters = [pl.ds(at, min(TILE, sums.shape[-1] - at)) for at in range(0, sums.shape[-1], TILE)]
     assert len(quarters) == PIECES
     gather_a = FarGather(along_z, lambda k, c, b: attn_all.at[k, b, c], ga_send, ga_recv)
     gather_b = Gather(along_x, lambda k, c, b: normed_all.at[k, c, b], gb_send, gb_recv)
     gather_c = PairGather(along_z, lambda k, c, b: hidden_all.at[k, c, b], gc_send, gc_recv)
-    scatter_a = PairScatter(along_x, lambda k: proj.at[k], (first_a, far_a, near_a, last_a), sa_send, sa_recv, halves)
+    scatter_a = PairScatter(along_x, lambda k: proj.at[k], (first_a, far_a, near_a, last_a), sa_send, sa_recv, whole)
     scatter_b = PairScatter(along_z, lambda k: sums.at[k % 2], (first_b, far_b, near_b, last_b), sb_send, sb_recv, quarters)
-    scatter_c = PairScatter(along_x, lambda k: proj.at[k], (first_c, far_c, near_c, last_c), sc_send, sc_recv, halves)
+    scatter_c = PairScatter(along_x, lambda k: proj.at[k], (first_c, far_c, near_c, last_c), sc_send, sc_recv, down_cuts)
 
     swaps = [
         remote(
@@ -540,7 +540,7 @@
             ),
             wo,
             proj.at[k],
-            side,
+            width,
             lambda j: scatter_a.step1(k, j),
         )
 
@@ -599,7 +599,7 @@
             lambda: jnp.concatenate([hidden_all[k, c].reshape(ROWS, half) for c in (0, 1)], axis=1),
             wd,
             proj.at[k],
-            side,
+            width // 2,
             lambda j: scatter_c.step1(k, j),
         )
 

time: 159 us -> 158 us (level)
  no operation moved by 1% of the time
where the time goes in v10:
time: 158 us
  Pallas kernels  155 us (98%)
  local copies, waits for them, and re-layouts  1.67 us (1%)
    pallas_call x1, Pallas kernels, layer(): pl.pallas_call(layer_kernel, out_shape=jax.ShapeDtypeStruct(resid.shape,...  155 us

profile of v10, /device:TPU:0, one launch (start us, length us, event | category | flops | bytes accessed | tf_op | source)
XLA Modules:
  0.0 158.3 jit_solution(1810067150748761373)
XLA Ops:
  1.3 155.3 %shard_map.127 = bf16[128,1024]{1,0:T(8,128)(2,1)} custom-call(s32[1,8]{1,0:T(1,128)} %page_table.1, s32[1]{0:T(128)S(6)} %copy.15.cache_len, s32[1]{0:T(128)S(6)} %copy.16.tree_size, s32[1,64]{1,0:T(1,128)} %parents.1, bf16[64,2048]{1,0:T(8,128)(2,1)} %queries_hbm.1, bf16[64,256]{1,0:T(8,128)(2,1)} %tree_kv_hbm.1, bf16[1,8,128,256]{3,2,1,0:T(8,128)(2,1)} %cache_hbm.1, ...), custom_call_target="tpu_custom_call" | custom-call | flops 25232932864 | bytes 27262976 | tf_op jit(solution)/shard_map/pallas_call | solution.py:705
  156.6 1.7 %copy.17 = bf16[128,1024]{1,0:T(8,128)(2,1)} copy(bf16[128,1024]{1,0:T(8,128)(2,1)} %shard_map.127) | data formatting | bytes 524288
